TPU v7x, 512 devices: a whole 4x4x16 slice. The times are simulated.
512 devices in a mesh: loop: 16 (over z_hi, x, core), rep: 32 (over z_lo, y).
Axes of the slice: x: 4, y: 4, z: 16 (z_hi: 2, z_lo: 8; z = z_hi * 8 + z_lo), core: 2. Of those that a mesh axis runs over, the one named last changes fastest.
Arguments:
- features: bfloat16 [3072, 32, 1152], P('loop', 'rep'), may hold values from -6 to 6
- text: bfloat16 [3072, 32, 1152], P('loop', 'rep'), may hold values from -6 to 6
- proj: bfloat16 [1152, 1152], replicated, may hold values from -0.1875 to 0.1875
- gain: float32 [1152], replicated, may hold values from 0.5 to 1.5
- scale: float32 [1], replicated, may hold values from 8 to 32
- bias: float32 [1], replicated, may hold values from -4 to 0
Outputs:
- feature_grad: bfloat16 [3072, 32, 1152], P('loop', 'rep')
- text_grad: bfloat16 [3072, 32, 1152], P('loop', 'rep')
- proj_grad: float32 [1152, 1152], P('rep')
- gain_gradient: float32 [1152], replicated
All inputs are finite; a program needn't handle non-finite values.
Results may differ from a plain program's by a relative error of at most 0.024.
Values may be sent and summed in bfloat16 or wider, within the bound.
A program may use at most 64 MiB of HBM per device.

v0:
```python
import jax
import jax.numpy as jnp
from jax import lax
from jax.sharding import PartitionSpec as P


def passed_along(value, axis, steps):
    count = lax.axis_size(axis)
    pairs = [(source, (source + steps) % count) for source in range(count)]
    return lax.ppermute(value, axis, pairs)


def unit_rows(values):
    inverse = lax.rsqrt(jnp.sum(values * values, axis=-1, keepdims=True) + 1e-06)
    return (values * inverse, inverse)


def local(features, text, proj, gain, scale, bias):
    loop_count = lax.axis_size("loop")
    row_count = features.shape[0]
    group_row_set = row_count * loop_count
    logit_scale = scale[0]
    logit_bias = bias[0]
    contract_last = (((1,), (1,)), ((), ()))
    contract_first = (((0,), (0,)), ((), ()))
    xvalues = features[:, 0, :].astype(jnp.float32)
    row_mean = jnp.mean(xvalues, axis=-1, keepdims=True)
    mean_removed = xvalues - row_mean
    row_inverse_deviation = lax.rsqrt(
        jnp.mean(mean_removed * mean_removed, axis=-1, keepdims=True) + 1e-06
    )
    standardized_input = mean_removed * row_inverse_deviation
    normalized_rows = (standardized_input * gain).astype(jnp.bfloat16)
    projected = jnp.dot(normalized_rows, proj, preferred_element_type=jnp.float32)
    img_dir, img_inv = unit_rows(projected)
    img_unit = img_dir.astype(jnp.bfloat16)
    txt_dir, txt_inv = unit_rows(text[:, 0, :].astype(jnp.float32))
    txt_unit = txt_dir.astype(jnp.bfloat16)
    empty = jnp.zeros((row_count, txt_unit.shape[1]), jnp.float32)
    local_ids = jnp.arange(row_count, dtype=jnp.int32)
    diag_mask = (local_ids[:, None] == local_ids[None, :]).astype(jnp.float32)

    def visit_step(turn_index, carry):
        visitor, text_sums, img_back = carry
        logits = (
            logit_scale
            * lax.dot_general(img_unit, visitor, contract_last, preferred_element_type=jnp.float32)
            + logit_bias
        )
        own_turn = (turn_index == 0).astype(jnp.float32)
        pair_weight = (jax.nn.sigmoid(logits) - own_turn * diag_mask).astype(jnp.bfloat16)
        img_back = img_back + logit_scale * jnp.dot(
            pair_weight, visitor, preferred_element_type=jnp.float32
        )
        text_sums = text_sums + logit_scale * lax.dot_general(
            pair_weight, img_unit, contract_first, preferred_element_type=jnp.float32
        )
        visitor = passed_along(visitor, "loop", 1)
        text_sums = passed_along(text_sums.astype(jnp.bfloat16), "loop", 1).astype(text_sums.dtype)
        return (visitor, text_sums, img_back)

    final_state = lax.fori_loop(0, loop_count, visit_step, (txt_unit, empty, empty))
    txt_back = final_state[1]
    img_back = final_state[2]
    proj_back = (
        (img_back - img_dir * jnp.sum(img_dir * img_back, axis=-1, keepdims=True)) * img_inv
    ).astype(jnp.bfloat16)
    text_out = (
        (txt_back - txt_dir * jnp.sum(txt_dir * txt_back, axis=-1, keepdims=True)) * txt_inv
    ).astype(jnp.bfloat16)
    norm_backward = lax.dot_general(
        proj_back, proj, contract_last, preferred_element_type=jnp.float32
    )
    scaled_backward = norm_backward * gain
    feature_result = (
        row_inverse_deviation
        * (
            scaled_backward
            - jnp.mean(scaled_backward, axis=-1, keepdims=True)
            - standardized_input
            * jnp.mean(scaled_backward * standardized_input, axis=-1, keepdims=True)
        )
    ).astype(jnp.bfloat16)
    partial_grad = lax.dot_general(
        normalized_rows, proj_back, contract_first, preferred_element_type=jnp.float32
    ) * (1.0 / group_row_set)
    row_block = lax.psum_scatter(
        partial_grad.astype(jnp.bfloat16), "rep", scatter_dimension=0, tiled=True
    )
    proj_grad = lax.psum(row_block, "loop").astype(jnp.float32)
    gain_gradient = lax.psum(
        jnp.sum(norm_backward * standardized_input, axis=0) * (1.0 / group_row_set), ("loop", "rep")
    )
    return (feature_result[:, None, :], text_out[:, None, :], proj_grad, gain_gradient)


def solution(mesh):
    return jax.shard_map(
        local,
        mesh=mesh,
        in_specs=(P("loop", "rep", None), P("loop", "rep", None), P(), P(), P(), P()),
        out_specs=(P("loop", "rep", None), P("loop", "rep", None), P("rep", None), P()),
        check_vma=False,
    )
```

profile of v0, /device:TPU:7, one launch (start us, length us, event | category | flops | bytes accessed | tf_op | source)
XLA Modules:
  0.0 1301.3 jit_solution(716019849992640693)
XLA Ops:
  15.0 840.3 %while.18 = (s32[]{:T(128)}, bf16[192,1152]{1,0:T(8,128)(2,1)}, f32[192,1152]{1,0:T(8,128)}, f32[192,1152]{1,0:T(8,128)}, f32[]{:T(128)}, /*index=5*/bf16[192,11...) while((s32[]{:T(128)}, bf16[192,1152]{1,0:T(8,128)(2,1)}, f32[192,1152]{1,0:T(8,128)}, ...), condition=%wide.region_5.0_spmd.clone, body=%wide.region_4.0_spmd.clone.sunk | while | flops 256905216 | bytes 14672137 | solution.py:62
  19.5 15.9 %collective-permute-start.1 = (bf16[192,1152]{1,0:T(8,128)(2,1)}, bf16[192,1152]{1,0:T(8,128)(2,1)}, u32[]{:S(2)}, u32[]{:S(2)}) collective-permute-start(bf16[192,1152]{1,0:T(8,128)(2,1)} %fusion.67), channel_id=1, source_target_pairs={{0,32},{32,64},{64,96},{96,128},{128,160},{160,192},{192,224},{224... | collective-permute-start | bytes 1327112 | tf_op jit(solution)/shard_map/while/body/eval_jaxpr/ppermute | solution.py:10
  40.2 9.1 collective-permute-done.1
  51.3 9.0 collective-permute-done
  64.8 15.8 %collective-permute-start.1 = (bf16[192,1152]{1,0:T(8,128)(2,1)}, bf16[192,1152]{1,0:T(8,128)(2,1)}, u32[]{:S(2)}, u32[]{:S(2)}) collective-permute-start(bf16[192,1152]{1,0:T(8,128)(2,1)} %fusion.67), channel_id=1, source_target_pairs={{0,32},{32,64},{64,96},{96,128},{128,160},{160,192},{192,224},{224... | collective-permute-start | bytes 1327112 | tf_op jit(solution)/shard_map/while/body/eval_jaxpr/ppermute | solution.py:10
  82.5 3.1 fusion.68
  88.8 30.4 %collective-permute-done = bf16[192,1152]{1,0:T(8,128)(2,1)} collective-permute-done((bf16[192,1152]{1,0:T(8,128)(2,1)S(1)}, bf16[192,1152]{1,0:T(8,128)(2,1)}, u32[]{:S(2)}, u32[]{:S(2)}) %collective-permute-start) | collective-permute-done | bytes 442400 | tf_op jit(solution)/shard_map/while/body/eval_jaxpr/ppermute | solution.py:10
  123.8 15.5 %collective-permute-start.1 = (bf16[192,1152]{1,0:T(8,128)(2,1)}, bf16[192,1152]{1,0:T(8,128)(2,1)}, u32[]{:S(2)}, u32[]{:S(2)}) collective-permute-start(bf16[192,1152]{1,0:T(8,128)(2,1)} %fusion.67), channel_id=1, source_target_pairs={{0,32},{32,64},{64,96},{96,128},{128,160},{160,192},{192,224},{224... | collective-permute-start | bytes 1327112 | tf_op jit(solution)/shard_map/while/body/eval_jaxpr/ppermute | solution.py:10
  141.1 3.1 fusion.68
  144.2 23.9 %collective-permute-done.1 = bf16[192,1152]{1,0:T(8,128)(2,1)} collective-permute-done((bf16[192,1152]{1,0:T(8,128)(2,1)}, bf16[192,1152]{1,0:T(8,128)(2,1)}, u32[]{:S(2)}, u32[]{:S(2)}) %collective-permute-start.1) | collective-permute-done | bytes 442400 | tf_op jit(solution)/shard_map/while/body/eval_jaxpr/ppermute | solution.py:10
  170.2 21.7 %collective-permute-done = bf16[192,1152]{1,0:T(8,128)(2,1)} collective-permute-done((bf16[192,1152]{1,0:T(8,128)(2,1)S(1)}, bf16[192,1152]{1,0:T(8,128)(2,1)}, u32[]{:S(2)}, u32[]{:S(2)}) %collective-permute-start) | collective-permute-done | bytes 442400 | tf_op jit(solution)/shard_map/while/body/eval_jaxpr/ppermute | solution.py:10
  196.4 15.4 %collective-permute-start.1 = (bf16[192,1152]{1,0:T(8,128)(2,1)}, bf16[192,1152]{1,0:T(8,128)(2,1)}, u32[]{:S(2)}, u32[]{:S(2)}) collective-permute-start(bf16[192,1152]{1,0:T(8,128)(2,1)} %fusion.67), channel_id=1, source_target_pairs={{0,32},{32,64},{64,96},{96,128},{128,160},{160,192},{192,224},{224... | collective-permute-start | bytes 1327112 | tf_op jit(solution)/shard_map/while/body/eval_jaxpr/ppermute | solution.py:10
  216.9 22.0 %collective-permute-done.1 = bf16[192,1152]{1,0:T(8,128)(2,1)} collective-permute-done((bf16[192,1152]{1,0:T(8,128)(2,1)}, bf16[192,1152]{1,0:T(8,128)(2,1)}, u32[]{:S(2)}, u32[]{:S(2)}) %collective-permute-start.1) | collective-permute-done | bytes 442400 | tf_op jit(solution)/shard_map/while/body/eval_jaxpr/ppermute | solution.py:10
  240.9 21.7 %collective-permute-done = bf16[192,1152]{1,0:T(8,128)(2,1)} collective-permute-done((bf16[192,1152]{1,0:T(8,128)(2,1)S(1)}, bf16[192,1152]{1,0:T(8,128)(2,1)}, u32[]{:S(2)}, u32[]{:S(2)}) %collective-permute-start) | collective-permute-done | bytes 442400 | tf_op jit(solution)/shard_map/while/body/eval_jaxpr/ppermute | solution.py:10
  267.1 15.4 %collective-permute-start.1 = (bf16[192,1152]{1,0:T(8,128)(2,1)}, bf16[192,1152]{1,0:T(8,128)(2,1)}, u32[]{:S(2)}, u32[]{:S(2)}) collective-permute-start(bf16[192,1152]{1,0:T(8,128)(2,1)} %fusion.67), channel_id=1, source_target_pairs={{0,32},{32,64},{64,96},{96,128},{128,160},{160,192},{192,224},{224... | collective-permute-start | bytes 1327112 | tf_op jit(solution)/shard_map/while/body/eval_jaxpr/ppermute | solution.py:10
  284.5 3.1 fusion.68
  287.6 22.1 %collective-permute-done.1 = bf16[192,1152]{1,0:T(8,128)(2,1)} collective-permute-done((bf16[192,1152]{1,0:T(8,128)(2,1)}, bf16[192,1152]{1,0:T(8,128)(2,1)}, u32[]{:S(2)}, u32[]{:S(2)}) %collective-permute-start.1) | collective-permute-done | bytes 442400 | tf_op jit(solution)/shard_map/while/body/eval_jaxpr/ppermute | solution.py:10
  311.6 21.7 %collective-permute-done = bf16[192,1152]{1,0:T(8,128)(2,1)} collective-permute-done((bf16[192,1152]{1,0:T(8,128)(2,1)S(1)}, bf16[192,1152]{1,0:T(8,128)(2,1)}, u32[]{:S(2)}, u32[]{:S(2)}) %collective-permute-start) | collective-permute-done | bytes 442400 | tf_op jit(solution)/shard_map/while/body/eval_jaxpr/ppermute | solution.py:10
  337.9 15.4 %collective-permute-start.1 = (bf16[192,1152]{1,0:T(8,128)(2,1)}, bf16[192,1152]{1,0:T(8,128)(2,1)}, u32[]{:S(2)}, u32[]{:S(2)}) collective-permute-start(bf16[192,1152]{1,0:T(8,128)(2,1)} %fusion.67), channel_id=1, source_target_pairs={{0,32},{32,64},{64,96},{96,128},{128,160},{160,192},{192,224},{224... | collective-permute-start | bytes 1327112 | tf_op jit(solution)/shard_map/while/body/eval_jaxpr/ppermute | solution.py:10
  358.3 22.0 %collective-permute-done.1 = bf16[192,1152]{1,0:T(8,128)(2,1)} collective-permute-done((bf16[192,1152]{1,0:T(8,128)(2,1)}, bf16[192,1152]{1,0:T(8,128)(2,1)}, u32[]{:S(2)}, u32[]{:S(2)}) %collective-permute-start.1) | collective-permute-done | bytes 442400 | tf_op jit(solution)/shard_map/while/body/eval_jaxpr/ppermute | solution.py:10
  382.3 21.7 %collective-permute-done = bf16[192,1152]{1,0:T(8,128)(2,1)} collective-permute-done((bf16[192,1152]{1,0:T(8,128)(2,1)S(1)}, bf16[192,1152]{1,0:T(8,128)(2,1)}, u32[]{:S(2)}, u32[]{:S(2)}) %collective-permute-start) | collective-permute-done | bytes 442400 | tf_op jit(solution)/shard_map/while/body/eval_jaxpr/ppermute | solution.py:10
  408.6 15.4 %collective-permute-start.1 = (bf16[192,1152]{1,0:T(8,128)(2,1)}, bf16[192,1152]{1,0:T(8,128)(2,1)}, u32[]{:S(2)}, u32[]{:S(2)}) collective-permute-start(bf16[192,1152]{1,0:T(8,128)(2,1)} %fusion.67), channel_id=1, source_target_pairs={{0,32},{32,64},{64,96},{96,128},{128,160},{160,192},{192,224},{224... | collective-permute-start | bytes 1327112 | tf_op jit(solution)/shard_map/while/body/eval_jaxpr/ppermute | solution.py:10
  429.0 22.0 %collective-permute-done.1 = bf16[192,1152]{1,0:T(8,128)(2,1)} collective-permute-done((bf16[192,1152]{1,0:T(8,128)(2,1)}, bf16[192,1152]{1,0:T(8,128)(2,1)}, u32[]{:S(2)}, u32[]{:S(2)}) %collective-permute-start.1) | collective-permute-done | bytes 442400 | tf_op jit(solution)/shard_map/while/body/eval_jaxpr/ppermute | solution.py:10
  453.0 21.7 %collective-permute-done = bf16[192,1152]{1,0:T(8,128)(2,1)} collective-permute-done((bf16[192,1152]{1,0:T(8,128)(2,1)S(1)}, bf16[192,1152]{1,0:T(8,128)(2,1)}, u32[]{:S(2)}, u32[]{:S(2)}) %collective-permute-start) | collective-permute-done | bytes 442400 | tf_op jit(solution)/shard_map/while/body/eval_jaxpr/ppermute | solution.py:10
  479.3 15.4 %collective-permute-start.1 = (bf16[192,1152]{1,0:T(8,128)(2,1)}, bf16[192,1152]{1,0:T(8,128)(2,1)}, u32[]{:S(2)}, u32[]{:S(2)}) collective-permute-start(bf16[192,1152]{1,0:T(8,128)(2,1)} %fusion.67), channel_id=1, source_target_pairs={{0,32},{32,64},{64,96},{96,128},{128,160},{160,192},{192,224},{224... | collective-permute-start | bytes 1327112 | tf_op jit(solution)/shard_map/while/body/eval_jaxpr/ppermute | solution.py:10
  499.7 22.0 %collective-permute-done.1 = bf16[192,1152]{1,0:T(8,128)(2,1)} collective-permute-done((bf16[192,1152]{1,0:T(8,128)(2,1)}, bf16[192,1152]{1,0:T(8,128)(2,1)}, u32[]{:S(2)}, u32[]{:S(2)}) %collective-permute-start.1) | collective-permute-done | bytes 442400 | tf_op jit(solution)/shard_map/while/body/eval_jaxpr/ppermute | solution.py:10
  523.7 21.7 %collective-permute-done = bf16[192,1152]{1,0:T(8,128)(2,1)} collective-permute-done((bf16[192,1152]{1,0:T(8,128)(2,1)S(1)}, bf16[192,1152]{1,0:T(8,128)(2,1)}, u32[]{:S(2)}, u32[]{:S(2)}) %collective-permute-start) | collective-permute-done | bytes 442400 | tf_op jit(solution)/shard_map/while/body/eval_jaxpr/ppermute | solution.py:10
  550.0 15.4 %collective-permute-start.1 = (bf16[192,1152]{1,0:T(8,128)(2,1)}, bf16[192,1152]{1,0:T(8,128)(2,1)}, u32[]{:S(2)}, u32[]{:S(2)}) collective-permute-start(bf16[192,1152]{1,0:T(8,128)(2,1)} %fusion.67), channel_id=1, source_target_pairs={{0,32},{32,64},{64,96},{96,128},{128,160},{160,192},{192,224},{224... | collective-permute-start | bytes 1327112 | tf_op jit(solution)/shard_map/while/body/eval_jaxpr/ppermute | solution.py:10
  567.3 3.1 fusion.68
  570.4 22.1 %collective-permute-done.1 = bf16[192,1152]{1,0:T(8,128)(2,1)} collective-permute-done((bf16[192,1152]{1,0:T(8,128)(2,1)}, bf16[192,1152]{1,0:T(8,128)(2,1)}, u32[]{:S(2)}, u32[]{:S(2)}) %collective-permute-start.1) | collective-permute-done | bytes 442400 | tf_op jit(solution)/shard_map/while/body/eval_jaxpr/ppermute | solution.py:10
  594.5 21.7 %collective-permute-done = bf16[192,1152]{1,0:T(8,128)(2,1)} collective-permute-done((bf16[192,1152]{1,0:T(8,128)(2,1)S(1)}, bf16[192,1152]{1,0:T(8,128)(2,1)}, u32[]{:S(2)}, u32[]{:S(2)}) %collective-permute-start) | collective-permute-done | bytes 442400 | tf_op jit(solution)/shard_map/while/body/eval_jaxpr/ppermute | solution.py:10
  620.7 15.4 %collective-permute-start.1 = (bf16[192,1152]{1,0:T(8,128)(2,1)}, bf16[192,1152]{1,0:T(8,128)(2,1)}, u32[]{:S(2)}, u32[]{:S(2)}) collective-permute-start(bf16[192,1152]{1,0:T(8,128)(2,1)} %fusion.67), channel_id=1, source_target_pairs={{0,32},{32,64},{64,96},{96,128},{128,160},{160,192},{192,224},{224... | collective-permute-start | bytes 1327112 | tf_op jit(solution)/shard_map/while/body/eval_jaxpr/ppermute | solution.py:10
  641.2 4.0 collective-permute-done.1
  654.3 15.4 %collective-permute-start.1 = (bf16[192,1152]{1,0:T(8,128)(2,1)}, bf16[192,1152]{1,0:T(8,128)(2,1)}, u32[]{:S(2)}, u32[]{:S(2)}) collective-permute-start(bf16[192,1152]{1,0:T(8,128)(2,1)} %fusion.67), channel_id=1, source_target_pairs={{0,32},{32,64},{64,96},{96,128},{128,160},{160,192},{192,224},{224... | collective-permute-start | bytes 1327112 | tf_op jit(solution)/shard_map/while/body/eval_jaxpr/ppermute | solution.py:10
  686.4 15.4 %collective-permute-start.1 = (bf16[192,1152]{1,0:T(8,128)(2,1)}, bf16[192,1152]{1,0:T(8,128)(2,1)}, u32[]{:S(2)}, u32[]{:S(2)}) collective-permute-start(bf16[192,1152]{1,0:T(8,128)(2,1)} %fusion.67), channel_id=1, source_target_pairs={{0,32},{32,64},{64,96},{96,128},{128,160},{160,192},{192,224},{224... | collective-permute-start | bytes 1327112 | tf_op jit(solution)/shard_map/while/body/eval_jaxpr/ppermute | solution.py:10
  709.3 6.4 collective-permute-done
  720.2 15.4 %collective-permute-start.1 = (bf16[192,1152]{1,0:T(8,128)(2,1)}, bf16[192,1152]{1,0:T(8,128)(2,1)}, u32[]{:S(2)}, u32[]{:S(2)}) collective-permute-start(bf16[192,1152]{1,0:T(8,128)(2,1)} %fusion.67), channel_id=1, source_target_pairs={{0,32},{32,64},{64,96},{96,128},{128,160},{160,192},{192,224},{224... | collective-permute-start | bytes 1327112 | tf_op jit(solution)/shard_map/while/body/eval_jaxpr/ppermute | solution.py:10
  743.2 12.0 collective-permute-done
  759.8 15.4 %collective-permute-start.1 = (bf16[192,1152]{1,0:T(8,128)(2,1)}, bf16[192,1152]{1,0:T(8,128)(2,1)}, u32[]{:S(2)}, u32[]{:S(2)}) collective-permute-start(bf16[192,1152]{1,0:T(8,128)(2,1)} %fusion.67), channel_id=1, source_target_pairs={{0,32},{32,64},{64,96},{96,128},{128,160},{160,192},{192,224},{224... | collective-permute-start | bytes 1327112 | tf_op jit(solution)/shard_map/while/body/eval_jaxpr/ppermute | solution.py:10
  780.2 7.5 collective-permute-done.1
  796.9 15.4 %collective-permute-start.1 = (bf16[192,1152]{1,0:T(8,128)(2,1)}, bf16[192,1152]{1,0:T(8,128)(2,1)}, u32[]{:S(2)}, u32[]{:S(2)}) collective-permute-start(bf16[192,1152]{1,0:T(8,128)(2,1)} %fusion.67), channel_id=1, source_target_pairs={{0,32},{32,64},{64,96},{96,128},{128,160},{160,192},{192,224},{224... | collective-permute-start | bytes 1327112 | tf_op jit(solution)/shard_map/while/body/eval_jaxpr/ppermute | solution.py:10
  828.3 15.4 %collective-permute-start.1 = (bf16[192,1152]{1,0:T(8,128)(2,1)}, bf16[192,1152]{1,0:T(8,128)(2,1)}, u32[]{:S(2)}, u32[]{:S(2)}) collective-permute-start(bf16[192,1152]{1,0:T(8,128)(2,1)} %fusion.67), channel_id=1, source_target_pairs={{0,32},{32,64},{64,96},{96,128},{128,160},{160,192},{192,224},{224... | collective-permute-start | bytes 1327112 | tf_op jit(solution)/shard_map/while/body/eval_jaxpr/ppermute | solution.py:10
  845.7 3.1 fusion.68
  861.3 121.7 %fusion.2 = bf16[48,1152]{1,0:T(8,128)(2,1)} fusion(bf16[1152,1152]{1,0:T(8,128)(2,1)} %fusion.13), kind=kCustom, calls=%all-reduce-scatter | all-reduce-scatter fusion | flops 1769473 | bytes 2766848
  998.9 10.2 collective-permute-start.8
  1012.2 14.0 %concatenate = bf16[420,1152]{1,0:T(8,128)(2,1)} concatenate(bf16[36,1152]{1,0:T(8,128)(2,1)} %copy-done.10, bf16[48,1152]{1,0:T(8,128)(2,1)S(1)} %collective-permute-done.8, bf16[48,1152]{1,0:T(8,128)(2,1)S(1)} %collective-permute-done.7, bf16[48,1152]{1,0:T(8,128)(2,1)S(1)} %collective-permute-done.6, bf16[48,1152]{1,0:T(8,128)(2,1)} %collective-permute-done.5, ...), dimensions={0} | concatenate | bytes 1935360
  1027.8 121.6 %psum.15 = f32[1152]{0:T(1024)} all-reduce(f32[1152]{0:T(1024)S(1)} %broadcast_multiply_fusion), channel_id=1, replica_groups=mesh['loop'=16,'rep'=32] {'loop','rep'}, use_global_device_ids=true, to_apply=%region_13.0 | all-reduce | flops 1152 | bytes 9216 | tf_op jit(solution)/shard_map/psum | solution.py:91
  1149.4 143.5 %all-reduce.4.cloned.1.call-done = bf16[36,1152]{1,0:T(8,128)(2,1)} async-done(((bf16[36,1152]{1,0:T(8,128)(2,1)}), bf16[36,1152]{1,0:T(8,128)(2,1)}) %all-reduce.4.cloned.1.call-update) | async-done | bytes 82960 | tf_op jit(solution)/shard_map/psum | solution.py:90
  (232 shorter events, 225.3 us)
Async XLA Ops:
  7.2 1285.7 %all-reduce.4.cloned.1.call-start = ((), (), s32[]{:S(2)}) async-start(), calls=%async_computation | async-start | bytes 184320 | tf_op jit(solution)/shard_map/psum | solution.py:90
  19.5 29.8 %collective-permute-start.1 = (bf16[192,1152]{1,0:T(8,128)(2,1)}, bf16[192,1152]{1,0:T(8,128)(2,1)}, u32[]{:S(2)}, u32[]{:S(2)}) collective-permute-start(bf16[192,1152]{1,0:T(8,128)(2,1)} %fusion.67), channel_id=1, source_target_pairs={{0,32},{32,64},{64,96},{96,128},{128,160},{160,192},{192,224},{224... | collective-permute-start | bytes 1327112 | tf_op jit(solution)/shard_map/while/body/eval_jaxpr/ppermute | solution.py:10
  35.5 24.8 %collective-permute-start = (bf16[192,1152]{1,0:T(8,128)(2,1)S(1)}, bf16[192,1152]{1,0:T(8,128)(2,1)}, u32[]{:S(2)}, u32[]{:S(2)}) collective-permute-start(bf16[192,1152]{1,0:T(8,128)(2,1)S(1)} %copy.15), channel_id=1, source_target_pairs={{0,32},{32,64},{64,96},{96,128},{128,160},{160,192},{192,224},{224... | collective-permute-start | bytes 1327112 | tf_op jit(solution)/shard_map/while/body/eval_jaxpr/ppermute | solution.py:10
  64.8 22.0 %collective-permute-start.1 = (bf16[192,1152]{1,0:T(8,128)(2,1)}, bf16[192,1152]{1,0:T(8,128)(2,1)}, u32[]{:S(2)}, u32[]{:S(2)}) collective-permute-start(bf16[192,1152]{1,0:T(8,128)(2,1)} %fusion.67), channel_id=1, source_target_pairs={{0,32},{32,64},{64,96},{96,128},{128,160},{160,192},{192,224},{224... | collective-permute-start | bytes 1327112 | tf_op jit(solution)/shard_map/while/body/eval_jaxpr/ppermute | solution.py:10
  80.6 38.6 %collective-permute-start = (bf16[192,1152]{1,0:T(8,128)(2,1)S(1)}, bf16[192,1152]{1,0:T(8,128)(2,1)}, u32[]{:S(2)}, u32[]{:S(2)}) collective-permute-start(bf16[192,1152]{1,0:T(8,128)(2,1)S(1)} %copy.15), channel_id=1, source_target_pairs={{0,32},{32,64},{64,96},{96,128},{128,160},{160,192},{192,224},{224... | collective-permute-start | bytes 1327112 | tf_op jit(solution)/shard_map/while/body/eval_jaxpr/ppermute | solution.py:10
  123.8 44.4 %collective-permute-start.1 = (bf16[192,1152]{1,0:T(8,128)(2,1)}, bf16[192,1152]{1,0:T(8,128)(2,1)}, u32[]{:S(2)}, u32[]{:S(2)}) collective-permute-start(bf16[192,1152]{1,0:T(8,128)(2,1)} %fusion.67), channel_id=1, source_target_pairs={{0,32},{32,64},{64,96},{96,128},{128,160},{160,192},{192,224},{224... | collective-permute-start | bytes 1327112 | tf_op jit(solution)/shard_map/while/body/eval_jaxpr/ppermute | solution.py:10
  139.2 52.7 %collective-permute-start = (bf16[192,1152]{1,0:T(8,128)(2,1)S(1)}, bf16[192,1152]{1,0:T(8,128)(2,1)}, u32[]{:S(2)}, u32[]{:S(2)}) collective-permute-start(bf16[192,1152]{1,0:T(8,128)(2,1)S(1)} %copy.15), channel_id=1, source_target_pairs={{0,32},{32,64},{64,96},{96,128},{128,160},{160,192},{192,224},{224... | collective-permute-start | bytes 1327112 | tf_op jit(solution)/shard_map/while/body/eval_jaxpr/ppermute | solution.py:10
  196.4 42.5 %collective-permute-start.1 = (bf16[192,1152]{1,0:T(8,128)(2,1)}, bf16[192,1152]{1,0:T(8,128)(2,1)}, u32[]{:S(2)}, u32[]{:S(2)}) collective-permute-start(bf16[192,1152]{1,0:T(8,128)(2,1)} %fusion.67), channel_id=1, source_target_pairs={{0,32},{32,64},{64,96},{96,128},{128,160},{160,192},{192,224},{224... | collective-permute-start | bytes 1327112 | tf_op jit(solution)/shard_map/while/body/eval_jaxpr/ppermute | solution.py:10
  211.8 50.7 %collective-permute-start = (bf16[192,1152]{1,0:T(8,128)(2,1)S(1)}, bf16[192,1152]{1,0:T(8,128)(2,1)}, u32[]{:S(2)}, u32[]{:S(2)}) collective-permute-start(bf16[192,1152]{1,0:T(8,128)(2,1)S(1)} %copy.15), channel_id=1, source_target_pairs={{0,32},{32,64},{64,96},{96,128},{128,160},{160,192},{192,224},{224... | collective-permute-start | bytes 1327112 | tf_op jit(solution)/shard_map/while/body/eval_jaxpr/ppermute | solution.py:10
  267.1 42.5 %collective-permute-start.1 = (bf16[192,1152]{1,0:T(8,128)(2,1)}, bf16[192,1152]{1,0:T(8,128)(2,1)}, u32[]{:S(2)}, u32[]{:S(2)}) collective-permute-start(bf16[192,1152]{1,0:T(8,128)(2,1)} %fusion.67), channel_id=1, source_target_pairs={{0,32},{32,64},{64,96},{96,128},{128,160},{160,192},{192,224},{224... | collective-permute-start | bytes 1327112 | tf_op jit(solution)/shard_map/while/body/eval_jaxpr/ppermute | solution.py:10
  282.5 50.8 %collective-permute-start = (bf16[192,1152]{1,0:T(8,128)(2,1)S(1)}, bf16[192,1152]{1,0:T(8,128)(2,1)}, u32[]{:S(2)}, u32[]{:S(2)}) collective-permute-start(bf16[192,1152]{1,0:T(8,128)(2,1)S(1)} %copy.15), channel_id=1, source_target_pairs={{0,32},{32,64},{64,96},{96,128},{128,160},{160,192},{192,224},{224... | collective-permute-start | bytes 1327112 | tf_op jit(solution)/shard_map/while/body/eval_jaxpr/ppermute | solution.py:10
  337.9 42.5 %collective-permute-start.1 = (bf16[192,1152]{1,0:T(8,128)(2,1)}, bf16[192,1152]{1,0:T(8,128)(2,1)}, u32[]{:S(2)}, u32[]{:S(2)}) collective-permute-start(bf16[192,1152]{1,0:T(8,128)(2,1)} %fusion.67), channel_id=1, source_target_pairs={{0,32},{32,64},{64,96},{96,128},{128,160},{160,192},{192,224},{224... | collective-permute-start | bytes 1327112 | tf_op jit(solution)/shard_map/while/body/eval_jaxpr/ppermute | solution.py:10
  353.3 50.7 %collective-permute-start = (bf16[192,1152]{1,0:T(8,128)(2,1)S(1)}, bf16[192,1152]{1,0:T(8,128)(2,1)}, u32[]{:S(2)}, u32[]{:S(2)}) collective-permute-start(bf16[192,1152]{1,0:T(8,128)(2,1)S(1)} %copy.15), channel_id=1, source_target_pairs={{0,32},{32,64},{64,96},{96,128},{128,160},{160,192},{192,224},{224... | collective-permute-start | bytes 1327112 | tf_op jit(solution)/shard_map/while/body/eval_jaxpr/ppermute | solution.py:10
  408.6 42.5 %collective-permute-start.1 = (bf16[192,1152]{1,0:T(8,128)(2,1)}, bf16[192,1152]{1,0:T(8,128)(2,1)}, u32[]{:S(2)}, u32[]{:S(2)}) collective-permute-start(bf16[192,1152]{1,0:T(8,128)(2,1)} %fusion.67), channel_id=1, source_target_pairs={{0,32},{32,64},{64,96},{96,128},{128,160},{160,192},{192,224},{224... | collective-permute-start | bytes 1327112 | tf_op jit(solution)/shard_map/while/body/eval_jaxpr/ppermute | solution.py:10
  424.0 50.7 %collective-permute-start = (bf16[192,1152]{1,0:T(8,128)(2,1)S(1)}, bf16[192,1152]{1,0:T(8,128)(2,1)}, u32[]{:S(2)}, u32[]{:S(2)}) collective-permute-start(bf16[192,1152]{1,0:T(8,128)(2,1)S(1)} %copy.15), channel_id=1, source_target_pairs={{0,32},{32,64},{64,96},{96,128},{128,160},{160,192},{192,224},{224... | collective-permute-start | bytes 1327112 | tf_op jit(solution)/shard_map/while/body/eval_jaxpr/ppermute | solution.py:10
  479.3 42.5 %collective-permute-start.1 = (bf16[192,1152]{1,0:T(8,128)(2,1)}, bf16[192,1152]{1,0:T(8,128)(2,1)}, u32[]{:S(2)}, u32[]{:S(2)}) collective-permute-start(bf16[192,1152]{1,0:T(8,128)(2,1)} %fusion.67), channel_id=1, source_target_pairs={{0,32},{32,64},{64,96},{96,128},{128,160},{160,192},{192,224},{224... | collective-permute-start | bytes 1327112 | tf_op jit(solution)/shard_map/while/body/eval_jaxpr/ppermute | solution.py:10
  494.7 50.8 %collective-permute-start = (bf16[192,1152]{1,0:T(8,128)(2,1)S(1)}, bf16[192,1152]{1,0:T(8,128)(2,1)}, u32[]{:S(2)}, u32[]{:S(2)}) collective-permute-start(bf16[192,1152]{1,0:T(8,128)(2,1)S(1)} %copy.15), channel_id=1, source_target_pairs={{0,32},{32,64},{64,96},{96,128},{128,160},{160,192},{192,224},{224... | collective-permute-start | bytes 1327112 | tf_op jit(solution)/shard_map/while/body/eval_jaxpr/ppermute | solution.py:10
  550.0 42.5 %collective-permute-start.1 = (bf16[192,1152]{1,0:T(8,128)(2,1)}, bf16[192,1152]{1,0:T(8,128)(2,1)}, u32[]{:S(2)}, u32[]{:S(2)}) collective-permute-start(bf16[192,1152]{1,0:T(8,128)(2,1)} %fusion.67), channel_id=1, source_target_pairs={{0,32},{32,64},{64,96},{96,128},{128,160},{160,192},{192,224},{224... | collective-permute-start | bytes 1327112 | tf_op jit(solution)/shard_map/while/body/eval_jaxpr/ppermute | solution.py:10
  565.4 50.8 %collective-permute-start = (bf16[192,1152]{1,0:T(8,128)(2,1)S(1)}, bf16[192,1152]{1,0:T(8,128)(2,1)}, u32[]{:S(2)}, u32[]{:S(2)}) collective-permute-start(bf16[192,1152]{1,0:T(8,128)(2,1)S(1)} %copy.15), channel_id=1, source_target_pairs={{0,32},{32,64},{64,96},{96,128},{128,160},{160,192},{192,224},{224... | collective-permute-start | bytes 1327112 | tf_op jit(solution)/shard_map/while/body/eval_jaxpr/ppermute | solution.py:10
  620.7 24.4 %collective-permute-start.1 = (bf16[192,1152]{1,0:T(8,128)(2,1)}, bf16[192,1152]{1,0:T(8,128)(2,1)}, u32[]{:S(2)}, u32[]{:S(2)}) collective-permute-start(bf16[192,1152]{1,0:T(8,128)(2,1)} %fusion.67), channel_id=1, source_target_pairs={{0,32},{32,64},{64,96},{96,128},{128,160},{160,192},{192,224},{224... | collective-permute-start | bytes 1327112 | tf_op jit(solution)/shard_map/while/body/eval_jaxpr/ppermute | solution.py:10
  636.1 13.7 %collective-permute-start = (bf16[192,1152]{1,0:T(8,128)(2,1)S(1)}, bf16[192,1152]{1,0:T(8,128)(2,1)}, u32[]{:S(2)}, u32[]{:S(2)}) collective-permute-start(bf16[192,1152]{1,0:T(8,128)(2,1)S(1)} %copy.15), channel_id=1, source_target_pairs={{0,32},{32,64},{64,96},{96,128},{128,160},{160,192},{192,224},{224... | collective-permute-start | bytes 1327112 | tf_op jit(solution)/shard_map/while/body/eval_jaxpr/ppermute | solution.py:10
  654.3 22.9 %collective-permute-start.1 = (bf16[192,1152]{1,0:T(8,128)(2,1)}, bf16[192,1152]{1,0:T(8,128)(2,1)}, u32[]{:S(2)}, u32[]{:S(2)}) collective-permute-start(bf16[192,1152]{1,0:T(8,128)(2,1)} %fusion.67), channel_id=1, source_target_pairs={{0,32},{32,64},{64,96},{96,128},{128,160},{160,192},{192,224},{224... | collective-permute-start | bytes 1327112 | tf_op jit(solution)/shard_map/while/body/eval_jaxpr/ppermute | solution.py:10
  669.7 12.1 collective-permute-start
  686.4 21.0 %collective-permute-start.1 = (bf16[192,1152]{1,0:T(8,128)(2,1)}, bf16[192,1152]{1,0:T(8,128)(2,1)}, u32[]{:S(2)}, u32[]{:S(2)}) collective-permute-start(bf16[192,1152]{1,0:T(8,128)(2,1)} %fusion.67), channel_id=1, source_target_pairs={{0,32},{32,64},{64,96},{96,128},{128,160},{160,192},{192,224},{224... | collective-permute-start | bytes 1327112 | tf_op jit(solution)/shard_map/while/body/eval_jaxpr/ppermute | solution.py:10
  701.8 13.9 %collective-permute-start = (bf16[192,1152]{1,0:T(8,128)(2,1)S(1)}, bf16[192,1152]{1,0:T(8,128)(2,1)}, u32[]{:S(2)}, u32[]{:S(2)}) collective-permute-start(bf16[192,1152]{1,0:T(8,128)(2,1)S(1)} %copy.15), channel_id=1, source_target_pairs={{0,32},{32,64},{64,96},{96,128},{128,160},{160,192},{192,224},{224... | collective-permute-start | bytes 1327112 | tf_op jit(solution)/shard_map/while/body/eval_jaxpr/ppermute | solution.py:10
  720.2 21.0 %collective-permute-start.1 = (bf16[192,1152]{1,0:T(8,128)(2,1)}, bf16[192,1152]{1,0:T(8,128)(2,1)}, u32[]{:S(2)}, u32[]{:S(2)}) collective-permute-start(bf16[192,1152]{1,0:T(8,128)(2,1)} %fusion.67), channel_id=1, source_target_pairs={{0,32},{32,64},{64,96},{96,128},{128,160},{160,192},{192,224},{224... | collective-permute-start | bytes 1327112 | tf_op jit(solution)/shard_map/while/body/eval_jaxpr/ppermute | solution.py:10
  735.7 19.6 %collective-permute-start = (bf16[192,1152]{1,0:T(8,128)(2,1)S(1)}, bf16[192,1152]{1,0:T(8,128)(2,1)}, u32[]{:S(2)}, u32[]{:S(2)}) collective-permute-start(bf16[192,1152]{1,0:T(8,128)(2,1)S(1)} %copy.15), channel_id=1, source_target_pairs={{0,32},{32,64},{64,96},{96,128},{128,160},{160,192},{192,224},{224... | collective-permute-start | bytes 1327112 | tf_op jit(solution)/shard_map/while/body/eval_jaxpr/ppermute | solution.py:10
  759.8 27.9 %collective-permute-start.1 = (bf16[192,1152]{1,0:T(8,128)(2,1)}, bf16[192,1152]{1,0:T(8,128)(2,1)}, u32[]{:S(2)}, u32[]{:S(2)}) collective-permute-start(bf16[192,1152]{1,0:T(8,128)(2,1)} %fusion.67), channel_id=1, source_target_pairs={{0,32},{32,64},{64,96},{96,128},{128,160},{160,192},{192,224},{224... | collective-permute-start | bytes 1327112 | tf_op jit(solution)/shard_map/while/body/eval_jaxpr/ppermute | solution.py:10
  775.2 17.1 %collective-permute-start = (bf16[192,1152]{1,0:T(8,128)(2,1)S(1)}, bf16[192,1152]{1,0:T(8,128)(2,1)}, u32[]{:S(2)}, u32[]{:S(2)}) collective-permute-start(bf16[192,1152]{1,0:T(8,128)(2,1)S(1)} %copy.15), channel_id=1, source_target_pairs={{0,32},{32,64},{64,96},{96,128},{128,160},{160,192},{192,224},{224... | collective-permute-start | bytes 1327112 | tf_op jit(solution)/shard_map/while/body/eval_jaxpr/ppermute | solution.py:10
  796.9 22.3 %collective-permute-start.1 = (bf16[192,1152]{1,0:T(8,128)(2,1)}, bf16[192,1152]{1,0:T(8,128)(2,1)}, u32[]{:S(2)}, u32[]{:S(2)}) collective-permute-start(bf16[192,1152]{1,0:T(8,128)(2,1)} %fusion.67), channel_id=1, source_target_pairs={{0,32},{32,64},{64,96},{96,128},{128,160},{160,192},{192,224},{224... | collective-permute-start | bytes 1327112 | tf_op jit(solution)/shard_map/while/body/eval_jaxpr/ppermute | solution.py:10
  812.3 11.5 collective-permute-start
  828.3 22.3 %collective-permute-start.1 = (bf16[192,1152]{1,0:T(8,128)(2,1)}, bf16[192,1152]{1,0:T(8,128)(2,1)}, u32[]{:S(2)}, u32[]{:S(2)}) collective-permute-start(bf16[192,1152]{1,0:T(8,128)(2,1)} %fusion.67), channel_id=1, source_target_pairs={{0,32},{32,64},{64,96},{96,128},{128,160},{160,192},{192,224},{224... | collective-permute-start | bytes 1327112 | tf_op jit(solution)/shard_map/while/body/eval_jaxpr/ppermute | solution.py:10
  843.8 11.5 collective-permute-start
  858.7 124.4 %copy-start.7 = (bf16[192,1152]{1,0:T(8,128)(2,1)}, bf16[192,1152]{1,0:T(8,128)(2,1)S(1)}, u32[]{:S(2)}) copy-start(bf16[192,1152]{1,0:T(8,128)(2,1)S(1)} %multiply_convert_fusion) | copy-start | bytes 1327108
  983.1 11.8 copy-start.12
  983.1 14.5 %collective-permute-start.2 = (bf16[48,1152]{1,0:T(8,128)(2,1)}, bf16[48,1152]{1,0:T(8,128)(2,1)S(1)}, u32[]{:S(2)}, u32[]{:S(2)}) collective-permute-start(bf16[48,1152]{1,0:T(8,128)(2,1)} %fusion.2), channel_id=1, source_target_pairs={{0,1},{1,2},{2,3},{3,4},{4,5},{5,6},{6,7},{7,8},{8,9},{9,10},{10,1... | collective-permute-start | bytes 331784
  984.5 14.4 %collective-permute-start.3 = (bf16[48,1152]{1,0:T(8,128)(2,1)}, bf16[48,1152]{1,0:T(8,128)(2,1)S(1)}, u32[]{:S(2)}, u32[]{:S(2)}) collective-permute-start(bf16[48,1152]{1,0:T(8,128)(2,1)} %fusion.2), channel_id=1, source_target_pairs={{0,2},{1,3},{2,4},{3,5},{4,6},{5,7},{6,8},{7,9},{8,10},{9,11},{10,... | collective-permute-start | bytes 331784
  985.8 26.3 %collective-permute-start.4 = (bf16[48,1152]{1,0:T(8,128)(2,1)}, bf16[48,1152]{1,0:T(8,128)(2,1)}, u32[]{:S(2)}, u32[]{:S(2)}) collective-permute-start(bf16[48,1152]{1,0:T(8,128)(2,1)} %fusion.2), channel_id=1, source_target_pairs={{0,3},{1,4},{2,5},{3,6},{4,7},{5,8},{6,9},{7,10},{8,11},{9,12},{10... | collective-permute-start | bytes 331784
  987.7 24.4 %collective-permute-start.5 = (bf16[48,1152]{1,0:T(8,128)(2,1)}, bf16[48,1152]{1,0:T(8,128)(2,1)}, u32[]{:S(2)}, u32[]{:S(2)}) collective-permute-start(bf16[48,1152]{1,0:T(8,128)(2,1)} %fusion.2), channel_id=1, source_target_pairs={{0,4},{1,5},{2,6},{3,7},{4,8},{5,9},{6,10},{7,11},{8,12},{9,13},{1... | collective-permute-start | bytes 331784
  990.6 5.4 copy-start.2
  990.6 5.6 collective-permute-start.9
  996.0 31.8 %copy-start.13 = (f32[1152]{0:T(1024)S(1)}, f32[1152]{0:T(1024)}, u32[]{:S(2)}) copy-start(f32[1152]{0:T(1024)} %get-tuple-element.172) | copy-start | bytes 13828
  996.2 15.2 %copy-start.10 = (bf16[36,1152]{1,0:T(8,128)(2,1)}, bf16[36,1152]{1,0:T(8,128)(2,1)S(1)}, u32[]{:S(2)}) copy-start(bf16[36,1152]{1,0:T(8,128)(2,1)S(1)} %collective-permute-done.9) | copy-start | bytes 248836
  996.2 15.9 %collective-permute-start.6 = (bf16[48,1152]{1,0:T(8,128)(2,1)}, bf16[48,1152]{1,0:T(8,128)(2,1)S(1)}, u32[]{:S(2)}, u32[]{:S(2)}) collective-permute-start(bf16[48,1152]{1,0:T(8,128)(2,1)} %fusion.2), channel_id=1, source_target_pairs={{0,5},{1,6},{2,7},{3,8},{4,9},{5,10},{6,11},{7,12},{8,13},{9,14},{... | collective-permute-start | bytes 331784
  997.6 12.5 copy-start.8
  997.6 14.6 %collective-permute-start.7 = (bf16[48,1152]{1,0:T(8,128)(2,1)}, bf16[48,1152]{1,0:T(8,128)(2,1)S(1)}, u32[]{:S(2)}, u32[]{:S(2)}) collective-permute-start(bf16[48,1152]{1,0:T(8,128)(2,1)} %fusion.2), channel_id=1, source_target_pairs={{0,6},{1,7},{2,8},{3,9},{4,10},{5,11},{6,12},{7,13},{8,14},{9,15},... | collective-permute-start | bytes 331784
  998.9 11.2 copy-start.9
  998.9 13.3 %collective-permute-start.8 = (bf16[48,1152]{1,0:T(8,128)(2,1)}, bf16[48,1152]{1,0:T(8,128)(2,1)S(1)}, u32[]{:S(2)}, u32[]{:S(2)}) collective-permute-start(bf16[48,1152]{1,0:T(8,128)(2,1)} %fusion.2), channel_id=1, source_target_pairs={{0,7},{1,8},{2,9},{3,10},{4,11},{5,12},{6,13},{7,14},{8,15},{9,16}... | collective-permute-start | bytes 331784
  (37 other events, 90.5 us)
Sparse Core Ops, SparseCore 0:
  1027.9 264.8 all-reduce.3
where the time goes:
time: 1310 us; the launch traced here: 1300 us
  waiting for transfers between devices  551 us (42%)
  starting transfers between devices  299 us (23%)
  blocking collectives  243 us (19%)
  matrix products  112 us (9%)
  other arithmetic  44.2 us (3%)
  local copies, waits for them, and re-layouts  35.6 us (3%)
  between operations  15 us (1%)
    ppermute x32, waiting for transfers between devices, passed_along(): return lax.ppermute(value, axis, pairs)  408 us
    ppermute x32, starting transfers between devices, passed_along(): return lax.ppermute(value, axis, pairs)  278 us
    psum x1, waiting for transfers between devices, local(): proj_grad = lax.psum(row_block, 'loop').astype(jnp.float32)  143 us
    unnamed x1, blocking collectives  122 us
    psum x1, blocking collectives, local(): lax.psum(jnp.sum(norm_backward * standardized_input, axis=0) * (1.0 / gro...  122 us
    dot_general x16, matrix products, visit_step(): jnp.dot(pair_weight, visitor, preferred_element_type=jnp.float32)  49.3 us
    convert_element_type x16, other arithmetic, visit_step(): passed_along(text_sums.astype(jnp.bfloat16), 'loop', 1)  32 us
    dot_general x16, matrix products, visit_step(): lax.dot_general(pair_weight, img_unit, contract_first, preferred_element_...  28.4 us
  transfers between devices with their start and end apart: 41, of which 33 were waited for; matrix products, arithmetic and copies ran while one was open for 7% of the time, Pallas kernels for 0%

commit v1 on v0

v1 whole, which is shorter than its diff:
```python
import functools

import jax
import jax.numpy as jnp
from jax import lax
from jax.experimental import pallas as pl
from jax.experimental.pallas import tpu as pltpu
from jax.sharding import PartitionSpec as P

MESH = pl.DeviceIdType.MESH
WIDTH = 1152
ROWS = 192
CHUNK = 48
CHUNKS = ROWS // CHUNK
PAIRS = 3072
TXT, IMG = 0, 1
OWN, FAR = 0, 1
WINDOW = 3
BLOCK_ROWS = 144
PIECE = 48
CUT = 640
LAST = (((1,), (1,)), ((), ()))
FIRST = (((0,), (0,)), ((), ()))
F32 = jnp.float32
BF16 = jnp.bfloat16


def coordinates():
    loop = lax.axis_index("loop")
    rep = lax.axis_index("rep")
    x = (loop // 2) % 4
    core = loop % 2
    z = (loop // 8) * 8 + rep // 4
    y = rep % 4
    return x, y, z, core


def device(x, y, z, core):
    x = (x + 4) % 4
    y = (y + 4) % 4
    z = (z + 32) % 16
    return ((z // 8) * 8 + x * 2 + core, (z % 8) * 4 + y)


def remote(src, dst, send_sem, recv_sem, target):
    return pltpu.make_async_remote_copy(
        src_ref=src,
        dst_ref=dst,
        send_sem=send_sem,
        recv_sem=recv_sem,
        device_id=target,
        device_id_type=MESH,
    )


def greet(peers):
    barrier = pltpu.get_barrier_semaphore()
    for peer in peers:
        pl.semaphore_signal(barrier, 1, device_id=peer, device_id_type=MESH)
    return lambda: pl.semaphore_wait(barrier, len(peers))


def row_sum(values):
    return jnp.sum(values, axis=-1, keepdims=True)


def pair_kernel(
    feat_ref, text_ref, proj_ref, gain_ref, scale_ref, bias_ref,
    feature_out, text_out, partial_out, gain_out,
    units, acc, xhat_ref, normed_ref, img_dir_ref, txt_dir_ref, row_ref,
    x_send, x_recv, s_send, s_recv, z_send, z_recv,
):
    x, y, z, core = coordinates()
    mine = x * 2 + core
    sibling = device(x, y, z, 1 - core)
    plus, minus = device(x + 1, y, z, core), device(x - 1, y, z, core)
    far = device(x, y, z + 8, core)
    finish_barrier = greet([sibling, plus, minus, far])
    scale = scale_ref[0]
    bias = bias_ref[0]

    def slot(steps, other=0):
        owner_core = core if other == 0 else 1 - core
        return ((x + steps) % 4) * 2 + owner_core

    def x_copy(arr, half, k, steps, src_slot, target):
        block = units.at[arr, half, k, src_slot]
        return remote(block, block, x_send.at[arr, half, k, steps], x_recv.at[arr, half, k, steps], target)

    def s_copy(arr, half, k, steps, from_sibling=0):
        block = units.at[arr, half, k, slot(steps, from_sibling)]
        return remote(block, block, s_send.at[arr, half, k, steps], s_recv.at[arr, half, k, steps], sibling)

    def z_copy(arr, k):
        return remote(
            units.at[arr, OWN, k, mine], units.at[arr, FAR, k, mine], z_send.at[arr, k], z_recv.at[arr, k], far
        )

    def plus_copy(arr, half, k):
        return x_copy(arr, half, k, 3, mine, plus)

    def minus_copy(arr, half, k):
        return x_copy(arr, half, k, 1, mine, minus)

    def onward_copy(arr, half, k):
        even = (k % 2) == 0
        steps = jnp.where(even, 3, 1)
        loop_id = jnp.where(even, plus[0], minus[0])
        return x_copy(arr, half, k, 2, slot(steps), (loop_id, plus[1]))

    def recv_x(arr, half, k, steps):
        x_copy(arr, half, k, steps, slot(steps), plus).wait_recv()

    def spread_own(arr, half, k):
        plus_copy(arr, half, k).start()
        minus_copy(arr, half, k).start()
        s_copy(arr, half, k, 0).start()

    def spread_neighbours(arr, half, k):
        recv_x(arr, half, k, 3)
        recv_x(arr, half, k, 1)
        onward_copy(arr, half, k).start()
        s_copy(arr, half, k, 3).start()
        s_copy(arr, half, k, 1).start()

    def spread_last(arr, half, k):
        recv_x(arr, half, k, 2)
        s_copy(arr, half, k, 2).start()

    def wait_sibling(arr, half, k):
        for steps in range(4):
            s_copy(arr, half, k, steps, 1).wait_recv()

    def wait_sends(arr, half, k):
        plus_copy(arr, half, k).wait_send()
        minus_copy(arr, half, k).wait_send()
        onward_copy(arr, half, k).wait_send()
        for steps in range(4):
            s_copy(arr, half, k, steps).wait_send()

    def attend(arr, half, k):
        own = units[1 - arr, OWN, :, mine].reshape(ROWS, WIDTH)
        keys = units[arr, half, k].reshape(8 * CHUNK, WIDTH)
        logits = scale * lax.dot_general(own, keys, LAST, preferred_element_type=F32) + bias
        weight = jax.nn.sigmoid(logits)
        if half == OWN:
            row = lax.broadcasted_iota(jnp.int32, weight.shape, 0)
            col = lax.broadcasted_iota(jnp.int32, weight.shape, 1)
            on = (col - mine * CHUNK == row - k * CHUNK) & (row >= k * CHUNK) & (row < (k + 1) * CHUNK)
            weight = weight - jnp.where(on, 1.0, 0.0)
        weight = weight.astype(BF16)
        acc[arr] += scale * jnp.dot(weight, keys, preferred_element_type=F32)

    def each(count, body):
        def step(k, carry):
            body(k)
            return carry

        lax.fori_loop(0, count, step, 0)

    acc[...] = jnp.zeros_like(acc)
    values = text_ref[...].astype(F32)
    txt_inv = lax.rsqrt(row_sum(values * values) + 1e-6)
    txt_dir = values * txt_inv
    txt_dir_ref[...] = txt_dir
    units[TXT, OWN, :, mine] = txt_dir.astype(BF16).reshape(CHUNKS, CHUNK, WIDTH)
    row_ref[0] = jnp.broadcast_to(txt_inv, (ROWS, 128))
    finish_barrier()
    for k in range(WINDOW):
        z_copy(TXT, k).start()
    each(CHUNKS, lambda k: spread_own(TXT, OWN, k))

    values = feat_ref[...].astype(F32)
    centred = values - row_sum(values) * (1.0 / WIDTH)
    deviation = lax.rsqrt(row_sum(centred * centred) * (1.0 / WIDTH) + 1e-6)
    row_ref[1] = jnp.broadcast_to(deviation, (ROWS, 128))
    xhat = centred * deviation
    xhat_ref[...] = xhat
    normed_ref[...] = (xhat * gain_ref[...]).astype(BF16)
    projected = jnp.dot(normed_ref[...], proj_ref[...], preferred_element_type=F32)
    img_inv = lax.rsqrt(row_sum(projected * projected) + 1e-6)
    row_ref[2] = jnp.broadcast_to(img_inv, (ROWS, 128))
    img_dir = projected * img_inv
    img_dir_ref[...] = img_dir
    units[IMG, OWN, :, mine] = img_dir.astype(BF16).reshape(CHUNKS, CHUNK, WIDTH)

    each(CHUNKS, lambda k: spread_neighbours(TXT, OWN, k))
    each(CHUNKS, lambda k: spread_last(TXT, OWN, k))

    def own_text(k):
        spread_own(IMG, OWN, k)
        wait_sibling(TXT, OWN, k)
        attend(TXT, OWN, k)

    each(CHUNKS, own_text)

    def far_text(k):
        z_copy(TXT, k).wait_recv()
        ahead = k + WINDOW

        @pl.when(ahead < CHUNKS)
        def _():
            z_copy(TXT, jnp.minimum(ahead, CHUNKS - 1)).start()

        @pl.when(ahead >= CHUNKS)
        def _():
            z_copy(IMG, jnp.maximum(ahead - CHUNKS, 0)).start()

        spread_own(TXT, FAR, k)
        spread_neighbours(IMG, OWN, k)
        spread_neighbours(TXT, FAR, k)
        spread_last(IMG, OWN, k)
        spread_last(TXT, FAR, k)
        wait_sibling(TXT, FAR, k)
        attend(TXT, FAR, k)
        wait_sibling(IMG, OWN, k)
        attend(IMG, OWN, k)

    each(CHUNKS, far_text)

    img_back = acc[TXT]
    img_dir = img_dir_ref[...]
    img_inv = row_ref[2][:, :1]
    proj_back = ((img_back - img_dir * row_sum(img_dir * img_back)) * img_inv).astype(BF16)
    partial = lax.dot_general(normed_ref[...], proj_back, FIRST, preferred_element_type=F32)
    partial_out[...] = (partial * (1.0 / PAIRS)).astype(BF16)
    norm_back = lax.dot_general(proj_back, proj_ref[...], LAST, preferred_element_type=F32)
    xhat = xhat_ref[...]
    deviation = row_ref[1][:, :1]
    gain_terms = (norm_back * xhat).reshape(ROWS // 8, 8, WIDTH)
    gain_out[...] = jnp.sum(gain_terms, axis=0) * (1.0 / PAIRS)
    scaled = norm_back * gain_ref[...]
    mean = row_sum(scaled) * (1.0 / WIDTH)
    along = row_sum(scaled * xhat) * (1.0 / WIDTH)
    feature_out[...] = (deviation * (scaled - mean - xhat * along)).astype(BF16)

    def far_image(k):
        z_copy(IMG, k).wait_recv()

        @pl.when(k + WINDOW < CHUNKS)
        def _():
            z_copy(IMG, jnp.minimum(k + WINDOW, CHUNKS - 1)).start()

        spread_own(IMG, FAR, k)
        spread_neighbours(IMG, FAR, k)
        spread_last(IMG, FAR, k)
        wait_sibling(IMG, FAR, k)
        attend(IMG, FAR, k)

    each(CHUNKS, far_image)

    txt_back = acc[IMG]
    txt_dir = txt_dir_ref[...]
    txt_inv = row_ref[0][:, :1]
    text_out[...] = ((txt_back - txt_dir * row_sum(txt_dir * txt_back)) * txt_inv).astype(BF16)

    def drain(k):
        for arr in (TXT, IMG):
            z_copy(arr, k).wait_send()
            for half in (OWN, FAR):
                wait_sends(arr, half, k)

    each(CHUNKS, drain)


def reduce_kernel(
    partial_ref, gain_ref, grad_out, gain_out,
    s_buf, summed, y_buf, y_sum, x_buf, x_sum, z_buf, gathered, g_sum, g_buf,
    s_send, s_recv, y_send, y_recv, x_send, x_recv, z_send, z_recv,
    b_send, b_recv, g_send, g_recv,
):
    x, y, z, core = coordinates()
    sibling = device(x, y, z, 1 - core)
    x_peers = [device(x + d, y, z, core) for d in (1, 2, 3)]
    y_peers = [device(x, y + d, z, core) for d in (1, 2, 3)]
    z_peers = [device(x, y, z + d, core) for d in range(1, 16)]
    greet([sibling] + x_peers + y_peers + z_peers)()

    def g_copies(stage, peers, base):
        return [
            remote(g_sum.at[stage], g_buf.at[base + i], g_send.at[base + i], g_recv.at[base + i], peer)
            for i, peer in enumerate(peers)
        ]

    def g_begin(stage, peers, base):
        for copy in g_copies(stage, peers, base):
            copy.start()

    def g_end(stage, peers, base):
        total = g_sum[stage]
        for i, copy in enumerate(g_copies(stage, peers, base)):
            copy.wait()
            total = total + g_buf[base + i]
        g_sum[stage + 1] = total

    z_quad = [device(x, y, z + 4 * d, core) for d in (1, 2, 3)]
    z_near = [device(x, y, (z // 4) * 4 + (z + d) % 4, core) for d in (1, 2, 3)]
    stages = [([sibling], 0), (y_peers, 1), (x_peers, 4), (z_quad, 7), (z_near, 10)]

    g_sum[0] = gain_ref[...]
    for j in range(4):
        rows = pl.ds(pl.multiple_of((1 - core) * 576 + j * BLOCK_ROWS, 16), BLOCK_ROWS)
        remote(partial_ref.at[rows], s_buf.at[j], s_send.at[j], s_recv.at[j], sibling).start()
    g_begin(0, *stages[0])

    def s_wait(j):
        return remote(partial_ref.at[pl.ds(0, BLOCK_ROWS)], s_buf.at[j], s_send.at[j], s_recv.at[j], sibling)

    def y_copy(j, d):
        rows = pl.ds(pl.multiple_of(((y + d) % 4) * 32, 16), PIECE)
        return remote(summed.at[j, rows], y_buf.at[d - 1, j], y_send.at[d - 1, j], y_recv.at[d - 1, j], y_peers[d - 1])

    for j in range(4):
        s_wait(j).wait_recv()
        rows = pl.ds(pl.multiple_of(core * 576 + j * BLOCK_ROWS, 16), BLOCK_ROWS)
        summed[j] = (partial_ref[rows].astype(F32) + s_buf[j].astype(F32)).astype(BF16)
        for d in (1, 2, 3):
            y_copy(j, d).start()
    g_end(0, *stages[0])
    g_begin(1, *stages[1])
    g_end(1, *stages[1])
    g_begin(2, *stages[2])

    here = pl.ds(pl.multiple_of(y * 32, 16), PIECE)
    for j in range(4):
        total = summed[j, here].astype(F32)
        for d in (1, 2, 3):
            y_copy(j, d).wait_recv()
            total = total + y_buf[d - 1, j].astype(F32)
        y_sum[j] = total.astype(BF16)

        @pl.when(x != j)
        def _():
            d = (j - x + 4) % 4
            remote(
                y_sum.at[j], x_buf.at[d - 1], x_send.at[d - 1], x_recv.at[d - 1], (device(j, y, z, core))
            ).start()

    g_end(2, *stages[2])
    g_begin(3, *stages[3])

    def x_wait(d):
        return remote(y_sum.at[0], x_buf.at[d - 1], x_send.at[d - 1], x_recv.at[d - 1], x_peers[0])

    total = y_sum[x].astype(F32)
    for d in (1, 2, 3):
        x_wait(d).wait_recv()
        total = total + x_buf[d - 1].astype(F32)
    x_sum[...] = total.astype(BF16)

    holder = core * 4 + x
    low, high = pl.ds(0, CUT), pl.ds(CUT, WIDTH - CUT)

    def z_copy(half, away):
        cols = low if half == 0 else high
        size = CUT if half == 0 else WIDTH - CUT
        return remote(
            x_sum.at[:, cols], z_buf.at[away - 1, :, pl.ds(0, size)], z_send.at[half], z_recv.at[away - 1],
            device(x, y, holder + 8 * half, core),
        )

    for half in (0, 1):
        away = (z - holder - 8 * half + 32) % 16

        @pl.when(away != 0)
        def _():
            z_copy(half, away).start()

    g_end(3, *stages[3])
    g_begin(4, *stages[4])

    def b1_copy(half):
        cols = low if half == 0 else high
        return remote(
            gathered.at[:, cols], gathered.at[:, cols], b_send.at[0], b_recv.at[0], device(x, y, z + 8, core)
        )

    is_holder = (z % 8) == holder
    for half in (0, 1):

        @pl.when(is_holder & (z // 8 == half))
        def _():
            size = CUT if half == 0 else WIDTH - CUT
            cols = low if half == 0 else high
            total = x_sum[:, cols].astype(F32)
            for away in range(1, 16):
                z_copy(half, away).wait_recv()
                total = total + z_buf[away - 1, :, pl.ds(0, size)].astype(F32)
            gathered[:, cols] = total.astype(BF16)
            b1_copy(half).start()
            b1_copy(1 - half).wait_recv()
            b1_copy(half).wait_send()

    def b2_copy(i):
        return remote(gathered, gathered, b_send.at[1 + i], b_recv.at[1], x_peers[i])

    def b3_copy():
        return remote(gathered, gathered, b_send.at[4], b_recv.at[1], sibling)

    root_core = (z % 8) // 4

    @pl.when(is_holder)
    def _():
        for i in range(3):
            b2_copy(i).start()

    @pl.when(jnp.logical_not(is_holder))
    def _():
        b2_copy(0).wait_recv()

    @pl.when(core == root_core)
    def _():
        b3_copy().start()

    g_end(4, *stages[4])
    gain_out[...] = jnp.sum(g_sum[5], axis=0, keepdims=True)

    @pl.when(is_holder)
    def _():
        for i in range(3):
            b2_copy(i).wait_send()

    @pl.when(core == root_core)
    def _():
        b3_copy().wait_send()

    grad_out[...] = gathered[...].astype(F32)
    for j in range(4):
        s_wait(j).wait_send()
        for d in (1, 2, 3):
            y_copy(j, d).wait_send()
    for d in (1, 2, 3):
        x_wait(d).wait_send()
    for half in (0, 1):
        away = (z - holder - 8 * half + 32) % 16

        @pl.when(away != 0)
        def _():
            z_copy(half, away).wait_send()


def local(features, text, proj, gain, scale, bias):
    vmem = pl.BlockSpec(memory_space=pltpu.VMEM)
    smem = pl.BlockSpec(memory_space=pltpu.SMEM)
    dma = pltpu.SemaphoreType.DMA
    feature_grad, text_grad, partial, gain_part = pl.pallas_call(
        pair_kernel,
        out_shape=[
            jax.ShapeDtypeStruct((ROWS, WIDTH), BF16),
            jax.ShapeDtypeStruct((ROWS, WIDTH), BF16),
            jax.ShapeDtypeStruct((WIDTH, WIDTH), BF16),
            jax.ShapeDtypeStruct((8, WIDTH), F32),
        ],
        in_specs=[vmem] * 4 + [smem] * 2,
        out_specs=[vmem] * 4,
        scratch_shapes=[
            pltpu.VMEM((2, 2, CHUNKS, 8, CHUNK, WIDTH), BF16),
            pltpu.VMEM((2, ROWS, WIDTH), F32),
            pltpu.VMEM((ROWS, WIDTH), F32),
            pltpu.VMEM((ROWS, WIDTH), BF16),
            pltpu.VMEM((ROWS, WIDTH), F32),
            pltpu.VMEM((ROWS, WIDTH), F32),
            pltpu.VMEM((3, ROWS, 128), F32),
            dma((2, 2, CHUNKS, 4)),
            dma((2, 2, CHUNKS, 4)),
            dma((2, 2, CHUNKS, 4)),
            dma((2, 2, CHUNKS, 4)),
            dma((2, CHUNKS)),
            dma((2, CHUNKS)),
        ],
        compiler_params=pltpu.CompilerParams(
            collective_id=0, has_side_effects=True, vmem_limit_bytes=60 * 2**20
        ),
        name="pairs",
    )(features[:, 0, :], text[:, 0, :], proj, gain[None, :], scale, bias)
    grad, gain_gradient = pl.pallas_call(
        reduce_kernel,
        out_shape=[
            jax.ShapeDtypeStruct((PIECE, WIDTH), F32),
            jax.ShapeDtypeStruct((1, WIDTH), F32),
        ],
        in_specs=[vmem] * 2,
        out_specs=[vmem] * 2,
        scratch_shapes=[
            pltpu.VMEM((4, BLOCK_ROWS, WIDTH), BF16),
            pltpu.VMEM((4, BLOCK_ROWS, WIDTH), BF16),
            pltpu.VMEM((3, 4, PIECE, WIDTH), BF16),
            pltpu.VMEM((4, PIECE, WIDTH), BF16),
            pltpu.VMEM((3, PIECE, WIDTH), BF16),
            pltpu.VMEM((PIECE, WIDTH), BF16),
            pltpu.VMEM((15, PIECE, CUT), BF16),
            pltpu.VMEM((PIECE, WIDTH), BF16),
            pltpu.VMEM((6, 8, WIDTH), F32),
            pltpu.VMEM((13, 8, WIDTH), F32),
            dma((4,)),
            dma((4,)),
            dma((3, 4)),
            dma((3, 4)),
            dma((3,)),
            dma((3,)),
            dma((2,)),
            dma((15,)),
            dma((5,)),
            dma((2,)),
            dma((13,)),
            dma((13,)),
        ],
        compiler_params=pltpu.CompilerParams(
            collective_id=1, has_side_effects=True, vmem_limit_bytes=60 * 2**20
        ),
        name="reduce",
    )(partial, gain_part)
    y = lax.axis_index("rep") % 4
    proj_grad = lax.dynamic_slice_in_dim(grad, y * 4, 36, 0)
    return feature_grad[:, None, :], text_grad[:, None, :], proj_grad, gain_gradient[0]


def solution(mesh):
    return jax.shard_map(
        local,
        mesh=mesh,
        in_specs=(P("loop", "rep", None), P("loop", "rep", None), P(), P(), P(), P()),
        out_specs=(P("loop", "rep", None), P("loop", "rep", None), P("rep", None), P()),
        check_vma=False,
    )
```

time: 1310 us -> 230 us (0.18)
  waiting for transfers between devices: 551 us -> 0 us
  starting transfers between devices: 299 us -> 0 us
  blocking collectives: 243 us -> 0 us
  Pallas kernels: 0 us -> 219 us
  matrix products: 112 us -> 0 us
  other arithmetic: 44.2 us -> 1.3 us
  local copies, waits for them, and re-layouts: 35.6 us -> 4.46 us
    ppermute x32 -> x0, waiting for transfers between devices: 408 us -> none  [passed_along(): return lax.ppermute(value, axis, pairs)]
    ppermute x32 -> x0, starting transfers between devices: 278 us -> none  [passed_along(): return lax.ppermute(value, axis, pairs)]
    pallas_call x0 -> x2, Pallas kernels: none -> 219 us  [the longest x1 142 us: local(): pl.pallas_call(pair_kernel, out_shape=[jax.ShapeDtypeStruct((ROWS, WIDTH)...]
    psum x1 -> x0, waiting for transfers between devices: 143 us -> none  [local(): proj_grad = lax.psum(row_block, 'loop').astype(jnp.float32)]
    unnamed x1 -> x0, blocking collectives: 122 us -> none
    psum x1 -> x0, blocking collectives: 122 us -> none  [local(): lax.psum(jnp.sum(norm_backward * standardized_input, axis=0) * (1.0 / gro...]
    dot_general x51 -> x0, matrix products: 112 us -> none  [the longest x16 49.3 us: visit_step(): jnp.dot(pair_weight, visitor, preferred_element_type=jnp.float32)]
    convert_element_type x19 -> x0, other arithmetic: 37.3 us -> none  [the longest x16 32 us: visit_step(): passed_along(text_sums.astype(jnp.bfloat16), 'loop', 1)]
  transfers between devices with their start and end apart: 41 -> 0, of which waited for: 33 -> 0; matrix products, arithmetic and copies ran while one was open for 7% -> 0% of each run, Pallas kernels for 0% -> 0%
where the time goes in v1:
time: 230 us; the launch traced here: 227 us
  Pallas kernels  219 us (95%)
  local copies, waits for them, and re-layouts  4.46 us (2%)
    pallas_call x1, Pallas kernels, local(): pl.pallas_call(pair_kernel, out_shape=[jax.ShapeDtypeStruct((ROWS, WIDTH)...  142 us
    pallas_call x1, Pallas kernels, local(): pl.pallas_call(reduce_kernel, out_shape=[jax.ShapeDtypeStruct((PIECE, WID...  77.5 us

profile of v1, /device:TPU:7, one launch (start us, length us, event | category | flops | bytes accessed | tf_op | source)
XLA Modules:
  0.0 227.2 jit_solution(6135769371943612204)
XLA Ops:
  0.6 1.3 broadcast_in_dim.9.gain_ref
  3.2 141.9 %pairs.1 = (bf16[192,1152]{1,0:T(8,128)(2,1)}, bf16[192,1152]{1,0:T(8,128)(2,1)}, bf16[1152,1152]{1,0:T(8,128)(2,1)}, f32[8,1152]{1,0:T(8,128)}) custom-call(bf16[192,1152]{1,0:T(8,128)(2,1)} %bitcast.4, bf16[192,1152]{1,0:T(8,128)(2,1)} %bitcast.5, bf16[1152,1152]{1,0:T(8,128)(2,1)} %proj_ref.1, f32[1,1152]{1,0:T(1,128)} %broadcast_in_dim.9.gain_ref, ...), custom_call_target="tpu_custom_call" | custom-call | tf_op jit(solution)/shard_map/pairs/pallas_call | solution.py:446
  145.2 0.0 copy-start.1
  145.2 0.0 copy-start
  145.2 77.5 %reduce.2 = (f32[48,1152]{1,0:T(8,128)}, f32[1,1152]{1,0:T(1,128)}) custom-call(bf16[1152,1152]{1,0:T(8,128)(2,1)} %get-tuple-element.12.partial_ref, f32[8,1152]{1,0:T(8,128)} %get-tuple-element.13.gain_ref), custom_call_target="tpu_custom_call" | custom-call | tf_op jit(solution)/shard_map/reduce/pallas_call | solution.py:476
  222.7 1.6 constant_dynamic-slice_fusion
  224.3 1.3 reduce.1
  225.6 0.0 copy-done.1
  225.6 0.8 copy.14
  226.4 0.0 copy-done
  226.4 0.8 copy.15
Async XLA Ops:
  145.2 80.5 %copy-start.1 = (bf16[192,1152]{1,0:T(8,128)(2,1)S(1)}, bf16[192,1152]{1,0:T(8,128)(2,1)}, u32[]{:S(2)}) copy-start(bf16[192,1152]{1,0:T(8,128)(2,1)} %get-tuple-element.10) | copy-start | bytes 1327108
  145.2 81.2 %copy-start = (bf16[192,1152]{1,0:T(8,128)(2,1)S(1)}, bf16[192,1152]{1,0:T(8,128)(2,1)}, u32[]{:S(2)}) copy-start(bf16[192,1152]{1,0:T(8,128)(2,1)} %get-tuple-element.11) | copy-start | bytes 1327108

commit v2 on v0

v2 whole, which is shorter than its diff:
```python
import functools

import jax
import jax.numpy as jnp
from jax import lax
from jax.experimental import pallas as pl
from jax.experimental.pallas import tpu as pltpu
from jax.sharding import PartitionSpec as P

MESH = pl.DeviceIdType.MESH
WIDTH = 1152
ROWS = 192
GRAIN = 16
GRAINS = ROWS // GRAIN
CHUNKS = (4, 4, 3, 1)
STARTS = (0, 4, 8, 11)
COUNT = len(CHUNKS)
PAIRS = 3072
TXT, IMG = 0, 1
OWN, FAR = 0, 1
WINDOW = 3
BLOCK_ROWS = 144
PIECE = 48
CUT = 512
REST = WIDTH - CUT
LAST = (((1,), (1,)), ((), ()))
FIRST = (((0,), (0,)), ((), ()))
F32 = jnp.float32
BF16 = jnp.bfloat16


def coordinates():
    loop = lax.axis_index("loop")
    rep = lax.axis_index("rep")
    x = (loop // 2) % 4
    core = loop % 2
    z = (loop // 8) * 8 + rep // 4
    y = rep % 4
    return x, y, z, core


def device(x, y, z, core):
    x = (x + 4) % 4
    y = (y + 4) % 4
    z = (z + 32) % 16
    return ((z // 8) * 8 + x * 2 + core, (z % 8) * 4 + y)


def remote(src, dst, send_sem, recv_sem, target):
    return pltpu.make_async_remote_copy(
        src_ref=src,
        dst_ref=dst,
        send_sem=send_sem,
        recv_sem=recv_sem,
        device_id=target,
        device_id_type=MESH,
    )


def greet(peers):
    barrier = pltpu.get_barrier_semaphore()
    for peer in peers:
        pl.semaphore_signal(barrier, 1, device_id=peer, device_id_type=MESH)
    return lambda: pl.semaphore_wait(barrier, len(peers))


def row_sum(values):
    return jnp.sum(values, axis=-1, keepdims=True)

ONWARD = (1, -1, 1, -1)
TXT_OWN = ((5.3, 10.3, 13.0), (8.7, 13.7, 16.7), (11.2, 16.2, 19.0), (12.0, 17.0, 20.0))
IMG_OWN = ((13.1, 21.0, 27.0, 30.0), (21.1, 28.0, 34.0, 37.0), (31.0, 38.0, 43.0, 58.0), (43.5, 51.0, 56.0, 60.0))
FAR_TIMES = (
    ((15.2, 20.5, 25.0, 28.0), (28.4, 33.5, 38.0, 40.0), (38.3, 43.0, 46.0, 47.0), (41.6, 44.0, 46.5, 48.0)),
    ((54.9, 60.0, 64.5, 67.5), (68.1, 73.0, 77.5, 79.5), (78.0, 82.5, 85.5, 87.0), (81.3, 83.5, 86.0, 88.0)),
)
TAIL = (49.0, 53.0, 56.0, 66.5, 67.0, 70.5, 72.0, 82.0, 86.2, 89.0)
GAIN_TIMES = (59.0, 62.0, 65.0, 70.0, 75.0)


def pair_kernel(
    feat_ref, text_ref, proj_ref, gain_ref, scale_ref, bias_ref,
    feature_out, text_out, grad_out, gain_out,
    units, acc, xhat_ref, normed_ref, normed_t, img_dir_ref, txt_dir_ref, row_ref, back_ref,
    theirs, summed, s_buf, ya_buf, ya_sum, xb_buf, xb_sum, xa_buf, yb_buf, part, z_buf, gathered, g_sum, g_buf,
    x_send, x_recv, s_send, s_recv, z_send, z_recv,
    c_send, c_recv, ya_send, ya_recv, xb_send, xb_recv, xa_send, xa_recv, yb_send, yb_recv,
    h_send, h_recv, b_send, b_recv, g_send, g_recv,
):
    x, y, z, core = coordinates()
    mine = x * 2 + core
    sibling = device(x, y, z, 1 - core)
    plus, minus = device(x + 1, y, z, core), device(x - 1, y, z, core)
    x_peers = [plus, device(x + 2, y, z, core), minus]
    y_peers = [device(x, y + d, z, core) for d in (1, 2, 3)]
    z_peers = [device(x, y, z + d, core) for d in range(1, 16)]
    z_quad = [device(x, y, z + 4 * d, core) for d in (1, 2, 3)]
    z_near = [device(x, y, (z // 4) * 4 + (z + d) % 4, core) for d in (1, 2, 3)]
    far = z_peers[7]
    finish_barrier = greet([sibling] + x_peers + y_peers + z_peers)
    scale = scale_ref[0]
    bias = bias_ref[0]
    started = []

    def go(copy):
        copy.start()
        started.append(copy)

    def slot(steps, other=0):
        owner_core = core if other == 0 else 1 - core
        return ((x + steps) % 4) * 2 + owner_core

    def block(arr, half, k, where):
        return units.at[arr, half, pl.ds(STARTS[k], CHUNKS[k]), where]

    def x_copy(arr, half, k, steps, where, target):
        ref = block(arr, half, k, where)
        return remote(ref, ref, x_send.at[arr, half, k, steps], x_recv.at[arr, half, k, steps], target)

    def s_copy(arr, half, k, steps, from_sibling=0):
        ref = block(arr, half, k, slot(steps, from_sibling))
        return remote(ref, ref, s_send.at[arr, half, k, steps], s_recv.at[arr, half, k, steps], sibling)

    def z_copy(arr, k):
        return remote(block(arr, OWN, k, mine), block(arr, FAR, k, mine), z_send.at[arr, k], z_recv.at[arr, k], far)

    def recv_x(arr, half, k, steps):
        x_copy(arr, half, k, steps, slot(steps), plus).wait_recv()

    def spread_own(arr, half, k):
        go(x_copy(arr, half, k, 3, mine, plus))
        go(x_copy(arr, half, k, 1, mine, minus))
        go(s_copy(arr, half, k, 0))

    def spread_neighbours(arr, half, k):
        recv_x(arr, half, k, 3)
        recv_x(arr, half, k, 1)
        if ONWARD[k] == 1:
            go(x_copy(arr, half, k, 2, slot(3), plus))
        else:
            go(x_copy(arr, half, k, 2, slot(1), minus))
        go(s_copy(arr, half, k, 3))
        go(s_copy(arr, half, k, 1))

    def spread_last(arr, half, k):
        recv_x(arr, half, k, 2)
        go(s_copy(arr, half, k, 2))

    def attend(arr, half, k):
        for steps in range(4):
            s_copy(arr, half, k, steps, 1).wait_recv()
        first, count = STARTS[k], CHUNKS[k]
        own = units[1 - arr, OWN, :, mine].reshape(ROWS, WIDTH)
        keys = units[arr, half, pl.ds(first, count)].reshape(count * 8 * GRAIN, WIDTH)
        logits = scale * lax.dot_general(own, keys, LAST, preferred_element_type=F32) + bias
        weight = jax.nn.sigmoid(logits)
        if half == OWN:
            row = lax.broadcasted_iota(jnp.int32, weight.shape, 0)
            col = lax.broadcasted_iota(jnp.int32, weight.shape, 1)
            grain = row // GRAIN
            match = (grain - first) * (8 * GRAIN) + mine * GRAIN + (row - grain * GRAIN)
            on = (col == match) & (grain >= first) & (grain < first + count)
            weight = weight - jnp.where(on, 1.0, 0.0)
        weight = weight.astype(BF16)
        acc[arr] += scale * jnp.dot(weight, keys, preferred_element_type=F32)

    crossing = [(arr, k) for arr in (TXT, IMG) for k in range(COUNT)]

    def arrive(i):
        z_copy(*crossing[i]).wait_recv()
        if i + WINDOW < len(crossing):
            go(z_copy(*crossing[i + WINDOW]))
        spread_own(crossing[i][0], FAR, crossing[i][1])

    def rows_of(who, j):
        return pl.ds(pl.multiple_of(who * 576 + j * BLOCK_ROWS, 16), BLOCK_ROWS)

    def half_copy(j):
        return remote(theirs.at[j], s_buf.at[j], c_send.at[j], c_recv.at[j], sibling)

    def product(who, j):
        return jnp.dot(normed_t[rows_of(who, j)], back_ref[...], preferred_element_type=F32) * (1.0 / PAIRS)

    def image_back():
        img_back = acc[TXT]
        img_dir = img_dir_ref[...]
        back_ref[...] = ((img_back - img_dir * row_sum(img_dir * img_back)) * row_ref[2][:, :1]).astype(BF16)
        for j in range(4):
            theirs[j] = product(1 - core, j).astype(BF16)
            go(half_copy(j))

    def y_rows(d):
        return pl.ds(pl.multiple_of(((y + d) % 4) * 32, 16), PIECE)

    low, high = pl.ds(0, CUT), pl.ds(CUT, REST)
    here = y_rows(0)

    def ya_copy(j, d):
        return remote(
            summed.at[j, y_rows(d), low], ya_buf.at[d - 1, j], ya_send.at[d - 1, j], ya_recv.at[d - 1, j], y_peers[d - 1]
        )

    def xb_copy(d):
        return remote(
            summed.at[(x + d) % 4, :, high], xb_buf.at[d - 1], xb_send.at[d - 1], xb_recv.at[d - 1], x_peers[d - 1]
        )

    def first_sums():
        for j in range(4):
            own = product(core, j)
            half_copy(j).wait_recv()
            summed[j] = (own + s_buf[j].astype(F32)).astype(BF16)
            for d in (2, 1, 3):
                go(ya_copy(j, d))
        for d in (2, 1, 3):
            go(xb_copy(d))

    def norm_back():
        value = lax.dot_general(back_ref[...], proj_ref[...], LAST, preferred_element_type=F32)
        xhat = xhat_ref[...]
        g_sum[0] = jnp.sum((value * xhat).reshape(ROWS // 8, 8, WIDTH), axis=0) * (1.0 / PAIRS)
        g_begin(0)
        scaled = value * gain_ref[...]
        mean = row_sum(scaled) * (1.0 / WIDTH)
        along = row_sum(scaled * xhat) * (1.0 / WIDTH)
        feature_out[...] = (row_ref[1][:, :1] * (scaled - mean - xhat * along)).astype(BF16)

    def xa_copy(d):
        return remote(ya_sum.at[(x + d) % 4], xa_buf.at[d - 1], xa_send.at[d - 1], xa_recv.at[d - 1], x_peers[d - 1])

    def yb_copy(d):
        return remote(xb_sum.at[y_rows(d)], yb_buf.at[d - 1], yb_send.at[d - 1], yb_recv.at[d - 1], y_peers[d - 1])

    def second_sums_b():
        total = summed[x, :, high].astype(F32)
        for d in (1, 2, 3):
            xb_copy(d).wait_recv()
            total = total + xb_buf[d - 1].astype(F32)
        xb_sum[...] = total.astype(BF16)
        for d in (2, 1, 3):
            go(yb_copy(d))

    def second_sums_a():
        for j in range(4):
            total = summed[j, here, low].astype(F32)
            for d in (1, 2, 3):
                ya_copy(j, d).wait_recv()
                total = total + ya_buf[d - 1, j].astype(F32)
            ya_sum[j] = total.astype(BF16)
        for d in (2, 1, 3):
            go(xa_copy(d))

    holder = core * 4 + x

    def h_copy(half, away):
        cols = low if half == 0 else high
        size = CUT if half == 0 else REST
        return remote(
            part.at[:, cols], z_buf.at[away - 1, :, pl.ds(0, size)], h_send.at[half], h_recv.at[away - 1],
            device(x, y, holder + 8 * half, core),
        )

    def away_from(half):
        return (z - holder - 8 * half + 32) % 16

    def to_holder(half):
        away = away_from(half)

        @pl.when(away != 0)
        def _():
            h_copy(half, away).start()

    def third_sums_b():
        total = xb_sum[here].astype(F32)
        for d in (1, 2, 3):
            yb_copy(d).wait_recv()
            total = total + yb_buf[d - 1].astype(F32)
        part[:, high] = total.astype(BF16)
        to_holder(1)

    def third_sums_a():
        total = ya_sum[x].astype(F32)
        for d in (1, 2, 3):
            xa_copy(d).wait_recv()
            total = total + xa_buf[d - 1].astype(F32)
        part[:, low] = total.astype(BF16)
        to_holder(0)

    is_holder = (z % 8) == holder
    on_root_core = core == (z % 8) // 4

    def cross_copy(half):
        cols = low if half == 0 else high
        return remote(gathered.at[:, cols], gathered.at[:, cols], b_send.at[0], b_recv.at[0], far)

    def row_copy(i):
        return remote(gathered, gathered, b_send.at[1 + i], b_recv.at[1], x_peers[i])

    def core_copy():
        return remote(gathered, gathered, b_send.at[4], b_recv.at[1], sibling)

    def holder_sums():
        for half in (0, 1):

            @pl.when(is_holder & (z // 8 == half))
            def _():
                size = CUT if half == 0 else REST
                cols = low if half == 0 else high
                total = part[:, cols].astype(F32)
                for away in range(1, 16):
                    h_copy(half, away).wait_recv()
                    total = total + z_buf[away - 1, :, pl.ds(0, size)].astype(F32)
                gathered[:, cols] = total.astype(BF16)
                cross_copy(half).start()

    def holder_rows():
        for half in (0, 1):

            @pl.when(is_holder & (z // 8 == half))
            def _():
                cross_copy(1 - half).wait_recv()
                cross_copy(half).wait_send()

        @pl.when(is_holder)
        def _():
            for i in (1, 0, 2):
                row_copy(i).start()
            core_copy().start()

    def spread_rows():
        @pl.when(jnp.logical_not(is_holder))
        def _():
            row_copy(0).wait_recv()

        @pl.when(on_root_core & jnp.logical_not(is_holder))
        def _():
            core_copy().start()

        grad_out[...] = gathered[...].astype(F32)

    stages = [([sibling], 0), (y_peers, 1), (x_peers, 4), (z_quad, 7), (z_near, 10)]

    def g_copies(stage):
        peers, base = stages[stage]
        return [
            remote(g_sum.at[stage], g_buf.at[base + i], g_send.at[base + i], g_recv.at[base + i], peer)
            for i, peer in enumerate(peers)
        ]

    def g_begin(stage):
        for copy in g_copies(stage):
            go(copy)

    def g_next(stage):
        total = g_sum[stage]
        for i, copy in enumerate(g_copies(stage)):
            copy.wait_recv()
            total = total + g_buf[stages[stage][1] + i]
        g_sum[stage + 1] = total
        if stage < 4:
            g_begin(stage + 1)
        else:
            gain_out[...] = jnp.sum(total, axis=0, keepdims=True)

    def text_back():
        txt_back = acc[IMG]
        txt_dir = txt_dir_ref[...]
        text_out[...] = ((txt_back - txt_dir * row_sum(txt_dir * txt_back)) * row_ref[0][:, :1]).astype(BF16)

    def text_units():
        values = text_ref[...].astype(F32)
        txt_inv = lax.rsqrt(row_sum(values * values) + 1e-6)
        txt_dir = values * txt_inv
        txt_dir_ref[...] = txt_dir
        units[TXT, OWN, :, mine] = txt_dir.astype(BF16).reshape(GRAINS, GRAIN, WIDTH)
        row_ref[0] = jnp.broadcast_to(txt_inv, (ROWS, 128))

    def image_units():
        values = feat_ref[...].astype(F32)
        centred = values - row_sum(values) * (1.0 / WIDTH)
        deviation = lax.rsqrt(row_sum(centred * centred) * (1.0 / WIDTH) + 1e-6)
        row_ref[1] = jnp.broadcast_to(deviation, (ROWS, 128))
        xhat = centred * deviation
        xhat_ref[...] = xhat
        normed_ref[...] = (xhat * gain_ref[...]).astype(BF16)
        projected = jnp.dot(normed_ref[...], proj_ref[...], preferred_element_type=F32)
        img_inv = lax.rsqrt(row_sum(projected * projected) + 1e-6)
        row_ref[2] = jnp.broadcast_to(img_inv, (ROWS, 128))
        img_dir = projected * img_inv
        img_dir_ref[...] = img_dir
        units[IMG, OWN, :, mine] = img_dir.astype(BF16).reshape(GRAINS, GRAIN, WIDTH)

    def transpose_normed():
        normed_t[...] = normed_ref[...].T

    acc[...] = jnp.zeros_like(acc)
    text_units()
    finish_barrier()
    for i in range(WINDOW):
        go(z_copy(*crossing[i]))
    for k in range(COUNT):
        spread_own(TXT, OWN, k)
    image_units()

    plan = [(9.0, transpose_normed, ())]

    def chain(arr, half, k, neighbours, last, pairs):
        plan.append((neighbours, spread_neighbours, (arr, half, k)))
        plan.append((last, spread_last, (arr, half, k)))
        plan.append((pairs, attend, (arr, half, k)))

    for k in range(COUNT):
        chain(TXT, OWN, k, *TXT_OWN[k])
        plan.append((IMG_OWN[k][0], spread_own, (IMG, OWN, k)))
        chain(IMG, OWN, k, *IMG_OWN[k][1:])
        for arr in (TXT, IMG):
            times = FAR_TIMES[arr][k]
            plan.append((times[0], arrive, (arr * COUNT + k,)))
            chain(arr, FAR, k, *times[1:])
    tail = [
        image_back, first_sums, norm_back, second_sums_b, second_sums_a, third_sums_b, third_sums_a,
        holder_sums, holder_rows, spread_rows,
    ]
    for time, work in zip(TAIL, tail):
        plan.append((time, work, ()))
    for stage in range(5):
        plan.append((GAIN_TIMES[stage], g_next, (stage,)))
    plan.append((200.0, text_back, ()))
    for _, work, args in sorted(plan, key=lambda entry: entry[0]):
        work(*args)

    for copy in started:
        copy.wait_send()
    for half in (0, 1):
        away = away_from(half)

        @pl.when(away != 0)
        def _():
            h_copy(half, away).wait_send()

    @pl.when(is_holder)
    def _():
        for i in range(3):
            row_copy(i).wait_send()

    @pl.when(on_root_core)
    def _():
        core_copy().wait_send()


def local(features, text, proj, gain, scale, bias):
    vmem = pl.BlockSpec(memory_space=pltpu.VMEM)
    smem = pl.BlockSpec(memory_space=pltpu.SMEM)
    dma = pltpu.SemaphoreType.DMA
    feature_grad, text_grad, grad, gain_gradient = pl.pallas_call(
        pair_kernel,
        out_shape=[
            jax.ShapeDtypeStruct((ROWS, WIDTH), BF16),
            jax.ShapeDtypeStruct((ROWS, WIDTH), BF16),
            jax.ShapeDtypeStruct((PIECE, WIDTH), F32),
            jax.ShapeDtypeStruct((1, WIDTH), F32),
        ],
        in_specs=[vmem] * 4 + [smem] * 2,
        out_specs=[vmem] * 4,
        scratch_shapes=[
            pltpu.VMEM((2, 2, GRAINS, 8, GRAIN, WIDTH), BF16),
            pltpu.VMEM((2, ROWS, WIDTH), F32),
            pltpu.VMEM((ROWS, WIDTH), F32),
            pltpu.VMEM((ROWS, WIDTH), BF16),
            pltpu.VMEM((WIDTH, ROWS), BF16),
            pltpu.VMEM((ROWS, WIDTH), F32),
            pltpu.VMEM((ROWS, WIDTH), F32),
            pltpu.VMEM((3, ROWS, 128), F32),
            pltpu.VMEM((ROWS, WIDTH), BF16),
            pltpu.VMEM((4, BLOCK_ROWS, WIDTH), BF16),
            pltpu.VMEM((4, BLOCK_ROWS, WIDTH), BF16),
            pltpu.VMEM((4, BLOCK_ROWS, WIDTH), BF16),
            pltpu.VMEM((3, 4, PIECE, CUT), BF16),
            pltpu.VMEM((4, PIECE, CUT), BF16),
            pltpu.VMEM((3, BLOCK_ROWS, REST), BF16),
            pltpu.VMEM((BLOCK_ROWS, REST), BF16),
            pltpu.VMEM((3, PIECE, CUT), BF16),
            pltpu.VMEM((3, PIECE, REST), BF16),
            pltpu.VMEM((PIECE, WIDTH), BF16),
            pltpu.VMEM((15, PIECE, REST), BF16),
            pltpu.VMEM((PIECE, WIDTH), BF16),
            pltpu.VMEM((6, 8, WIDTH), F32),
            pltpu.VMEM((13, 8, WIDTH), F32),
            dma((2, 2, COUNT, 4)),
            dma((2, 2, COUNT, 4)),
            dma((2, 2, COUNT, 4)),
            dma((2, 2, COUNT, 4)),
            dma((2, COUNT)),
            dma((2, COUNT)),
            dma((4,)),
            dma((4,)),
            dma((3, 4)),
            dma((3, 4)),
            dma((3,)),
            dma((3,)),
            dma((3,)),
            dma((3,)),
            dma((3,)),
            dma((3,)),
            dma((2,)),
            dma((15,)),
            dma((5,)),
            dma((2,)),
            dma((13,)),
            dma((13,)),
        ],
        compiler_params=pltpu.CompilerParams(
            collective_id=0, has_side_effects=True, vmem_limit_bytes=60 * 2**20
        ),
        name="pairs",
    )(features[:, 0, :], text[:, 0, :], proj, gain[None, :], scale, bias)
    y = lax.axis_index("rep") % 4
    proj_grad = lax.dynamic_slice_in_dim(grad, y * 4, 36, 0)
    return feature_grad[:, None, :], text_grad[:, None, :], proj_grad, gain_gradient[0]

def solution(mesh):
    return jax.shard_map(
        local,
        mesh=mesh,
        in_specs=(P("loop", "rep", None), P("loop", "rep", None), P(), P(), P(), P()),
        out_specs=(P("loop", "rep", None), P("loop", "rep", None), P("rep", None), P()),
        check_vma=False,
    )
```

time: 1310 us -> 162 us (0.12)
  waiting for transfers between devices: 551 us -> 0 us
  starting transfers between devices: 299 us -> 0 us
  blocking collectives: 243 us -> 0 us
  Pallas kernels: 0 us -> 150 us
  matrix products: 112 us -> 0 us
  other arithmetic: 44.2 us -> 1.3 us
  local copies, waits for them, and re-layouts: 35.6 us -> 6.55 us
    ppermute x32 -> x0, waiting for transfers between devices: 408 us -> none  [passed_along(): return lax.ppermute(value, axis, pairs)]
    ppermute x32 -> x0, starting transfers between devices: 278 us -> none  [passed_along(): return lax.ppermute(value, axis, pairs)]
    pallas_call x0 -> x1, Pallas kernels: none -> 150 us  [local(): pl.pallas_call(pair_kernel, out_shape=[jax.ShapeDtypeStruct((ROWS, WIDTH)...]
    psum x1 -> x0, waiting for transfers between devices: 143 us -> none  [local(): proj_grad = lax.psum(row_block, 'loop').astype(jnp.float32)]
    unnamed x1 -> x0, blocking collectives: 122 us -> none
    psum x1 -> x0, blocking collectives: 122 us -> none  [local(): lax.psum(jnp.sum(norm_backward * standardized_input, axis=0) * (1.0 / gro...]
    dot_general x51 -> x0, matrix products: 112 us -> none  [the longest x16 49.3 us: visit_step(): jnp.dot(pair_weight, visitor, preferred_element_type=jnp.float32)]
    convert_element_type x19 -> x0, other arithmetic: 37.3 us -> none  [the longest x16 32 us: visit_step(): passed_along(text_sums.astype(jnp.bfloat16), 'loop', 1)]
  transfers between devices with their start and end apart: 41 -> 0, of which waited for: 33 -> 0; matrix products, arithmetic and copies ran while one was open for 7% -> 0% of each run, Pallas kernels for 0% -> 0%
where the time goes in v2:
time: 162 us; the launch traced here: 160 us
  Pallas kernels  150 us (93%)
  local copies, waits for them, and re-layouts  6.55 us (4%)
  between operations  1.96 us (1%)
    pallas_call x1, Pallas kernels, local(): pl.pallas_call(pair_kernel, out_shape=[jax.ShapeDtypeStruct((ROWS, WIDTH)...  150 us
    unnamed x2, local copies, waits for them, and re-layouts  3.62 us

profile of v2, /device:TPU:7, one launch (start us, length us, event | category | flops | bytes accessed | tf_op | source)
XLA Modules:
  0.0 159.8 jit_solution(2311798373017843139)
XLA Ops:
  0.6 1.3 broadcast_in_dim.9.gain_ref
  3.2 150.0 %pairs.1 = (bf16[192,1152]{1,0:T(8,128)(2,1)}, bf16[192,1152]{1,0:T(8,128)(2,1)}, f32[48,1152]{1,0:T(8,128)}, f32[1,1152]{1,0:T(1,128)}) custom-call(bf16[192,1152]{1,0:T(8,128)(2,1)} %bitcast.4, bf16[192,1152]{1,0:T(8,128)(2,1)} %bitcast.5, bf16[1152,1152]{1,0:T(8,128)(2,1)} %proj_ref.1, f32[1,1152]{1,0:T(1,128)} %broadcast_in_dim.9.gain_ref, ...), custom_call_target="tpu_custom_call" | custom-call | tf_op jit(solution)/shard_map/pairs/pallas_call | solution.py:455
  153.3 1.6 %constant_dynamic-slice_fusion = f32[36,1152]{1,0:T(8,128)} fusion(f32[48,1152]{1,0:T(8,128)} %get-tuple-element.10, s32[]{:T(128)S(6)} %select_n.11), kind=kLoop, calls=%fused_computation | loop fusion | bytes 331780 | tf_op jit(solution)/shard_map/dynamic_slice | solution.py:518
  154.9 1.3 reduce
  156.2 1.8 %copy.14 = bf16[192,1,1152]{2,0,1:T(8,128)(2,1)} copy(bf16[192,1,1152]{2,0,1:T(8,128)(2,1)} %bitcast.7) | data formatting | bytes 884736
  158.0 1.8 %copy.15 = bf16[192,1,1152]{2,0,1:T(8,128)(2,1)} copy(bf16[192,1,1152]{2,0,1:T(8,128)(2,1)} %bitcast.6) | data formatting | bytes 884736

commit v3 on v2

--- a/solution.py
+++ b/solution.py
@@ -18,7 +18,7 @@
 PAIRS = 3072
 TXT, IMG = 0, 1
 OWN, FAR = 0, 1
-WINDOW = 3
+WINDOW = 2
 BLOCK_ROWS = 144
 PIECE = 48
 CUT = 512
@@ -69,13 +69,13 @@
 
 ONWARD = (1, -1, 1, -1)
 TXT_OWN = ((5.3, 10.3, 13.0), (8.7, 13.7, 16.7), (11.2, 16.2, 19.0), (12.0, 17.0, 20.0))
-IMG_OWN = ((13.1, 21.0, 27.0, 30.0), (21.1, 28.0, 34.0, 37.0), (31.0, 38.0, 43.0, 58.0), (43.5, 51.0, 56.0, 60.0))
+IMG_OWN = ((11.0, 20.0, 26.0, 30.0), (13.0, 23.0, 29.0, 33.0), (15.0, 26.0, 32.0, 36.0), (17.0, 28.0, 34.0, 39.0))
 FAR_TIMES = (
-    ((15.2, 20.5, 25.0, 28.0), (28.4, 33.5, 38.0, 40.0), (38.3, 43.0, 46.0, 47.0), (41.6, 44.0, 46.5, 48.0)),
-    ((54.9, 60.0, 64.5, 67.5), (68.1, 73.0, 77.5, 79.5), (78.0, 82.5, 85.5, 87.0), (81.3, 83.5, 86.0, 88.0)),
+    ((24.0, 30.0, 35.0, 38.0), (36.0, 40.5, 44.0, 46.5), (44.5, 48.0, 51.0, 53.5), (47.0, 49.5, 52.0, 54.0)),
+    ((69.0, 74.0, 78.5, 81.0), (76.0, 80.5, 84.5, 87.5), (82.0, 85.5, 88.3, 90.0), (84.0, 87.0, 89.5, 91.0)),
 )
-TAIL = (49.0, 53.0, 56.0, 66.5, 67.0, 70.5, 72.0, 82.0, 86.2, 89.0)
-GAIN_TIMES = (59.0, 62.0, 65.0, 70.0, 75.0)
+TAIL = (55.0, 58.0, 60.0, 66.0, 67.0, 71.0, 72.0, 86.0, 89.2, 92.0)
+GAIN_TIMES = (62.5, 67.5, 72.2, 90.5, 92.5)
 
 
 def pair_kernel(
@@ -94,8 +94,6 @@
     x_peers = [plus, device(x + 2, y, z, core), minus]
     y_peers = [device(x, y + d, z, core) for d in (1, 2, 3)]
     z_peers = [device(x, y, z + d, core) for d in range(1, 16)]
-    z_quad = [device(x, y, z + 4 * d, core) for d in (1, 2, 3)]
-    z_near = [device(x, y, (z // 4) * 4 + (z + d) % 4, core) for d in (1, 2, 3)]
     far = z_peers[7]
     finish_barrier = greet([sibling] + x_peers + y_peers + z_peers)
     scale = scale_ref[0]
@@ -168,8 +166,11 @@
 
     def arrive(i):
         z_copy(*crossing[i]).wait_recv()
-        if i + WINDOW < len(crossing):
+        if i + WINDOW < COUNT:
             go(z_copy(*crossing[i + WINDOW]))
+        if i == COUNT - 1:
+            for k in range(COUNT):
+                go(z_copy(IMG, k))
         spread_own(crossing[i][0], FAR, crossing[i][1])
 
     def rows_of(who, j):
@@ -218,8 +219,10 @@
     def norm_back():
         value = lax.dot_general(back_ref[...], proj_ref[...], LAST, preferred_element_type=F32)
         xhat = xhat_ref[...]
-        g_sum[0] = jnp.sum((value * xhat).reshape(ROWS // 8, 8, WIDTH), axis=0) * (1.0 / PAIRS)
-        g_begin(0)
+        terms = jnp.sum(value * xhat, axis=0, keepdims=True) * (1.0 / PAIRS)
+        for i in range(9):
+            g_sum[0, pl.ds(i, 1)] = terms[:, 128 * i : 128 * (i + 1)]
+        go(g_copies(0)[0])
         scaled = value * gain_ref[...]
         mean = row_sum(scaled) * (1.0 / WIDTH)
         along = row_sum(scaled * xhat) * (1.0 / WIDTH)
@@ -338,7 +341,7 @@
 
         grad_out[...] = gathered[...].astype(F32)
 
-    stages = [([sibling], 0), (y_peers, 1), (x_peers, 4), (z_quad, 7), (z_near, 10)]
+    stages = [([sibling], 0), (y_peers, 1), (x_peers, 4), (z_peers, 7)]
 
     def g_copies(stage):
         peers, base = stages[stage]
@@ -347,20 +350,41 @@
             for i, peer in enumerate(peers)
         ]
 
-    def g_begin(stage):
-        for copy in g_copies(stage):
-            go(copy)
-
-    def g_next(stage):
+    def g_total(stage):
         total = g_sum[stage]
         for i, copy in enumerate(g_copies(stage)):
             copy.wait_recv()
             total = total + g_buf[stages[stage][1] + i]
         g_sum[stage + 1] = total
-        if stage < 4:
-            g_begin(stage + 1)
+
+    def g_next(stage):
+        g_total(stage)
+        if stage < 2:
+            for copy in g_copies(stage + 1):
+                go(copy)
         else:
-            gain_out[...] = jnp.sum(total, axis=0, keepdims=True)
+
+            @pl.when(core == 0)
+            def _():
+                for copy in g_copies(3):
+                    copy.start()
+
+    def g_core_copy():
+        return remote(g_sum.at[4], g_sum.at[4], g_send.at[22], g_recv.at[22], sibling)
+
+    def g_along_z():
+        @pl.when(core == 0)
+        def _():
+            g_total(3)
+            g_core_copy().start()
+
+    def g_finish():
+        @pl.when(core == 1)
+        def _():
+            g_core_copy().wait_recv()
+
+        for i in range(9):
+            gain_out[:, pl.ds(128 * i, 128)] = g_sum[4, pl.ds(i, 1)]
 
     def text_back():
         txt_back = acc[IMG]
@@ -423,8 +447,10 @@
     ]
     for time, work in zip(TAIL, tail):
         plan.append((time, work, ()))
-    for stage in range(5):
+    for stage in range(3):
         plan.append((GAIN_TIMES[stage], g_next, (stage,)))
+    plan.append((GAIN_TIMES[3], g_along_z, ()))
+    plan.append((GAIN_TIMES[4], g_finish, ()))
     plan.append((200.0, text_back, ()))
     for _, work, args in sorted(plan, key=lambda entry: entry[0]):
         work(*args)
@@ -446,6 +472,12 @@
     @pl.when(on_root_core)
     def _():
         core_copy().wait_send()
+
+    @pl.when(core == 0)
+    def _():
+        for copy in g_copies(3):
+            copy.wait_send()
+        g_core_copy().wait_send()
 
 
 def local(features, text, proj, gain, scale, bias):
@@ -484,8 +516,8 @@
             pltpu.VMEM((PIECE, WIDTH), BF16),
             pltpu.VMEM((15, PIECE, REST), BF16),
             pltpu.VMEM((PIECE, WIDTH), BF16),
-            pltpu.VMEM((6, 8, WIDTH), F32),
-            pltpu.VMEM((13, 8, WIDTH), F32),
+            pltpu.VMEM((5, 9, 128), F32),
+            pltpu.VMEM((22, 9, 128), F32),
             dma((2, 2, COUNT, 4)),
             dma((2, 2, COUNT, 4)),
             dma((2, 2, COUNT, 4)),
@@ -506,8 +538,8 @@
             dma((15,)),
             dma((5,)),
             dma((2,)),
-            dma((13,)),
-            dma((13,)),
+            dma((23,)),
+            dma((23,)),
         ],
         compiler_params=pltpu.CompilerParams(
             collective_id=0, has_side_effects=True, vmem_limit_bytes=60 * 2**20

time: 162 us -> 149 us (0.920)
  Pallas kernels: 150 us -> 138 us
    pallas_call x1, Pallas kernels: 150 us -> 138 us  [local(): pl.pallas_call(pair_kernel, out_shape=[jax.ShapeDtypeStruct((ROWS, WIDTH)...]
where the time goes in v3:
time: 149 us; the launch traced here: 148 us
  Pallas kernels  138 us (93%)
  local copies, waits for them, and re-layouts  6.55 us (4%)
  between operations  1.96 us (1%)
    pallas_call x1, Pallas kernels, local(): pl.pallas_call(pair_kernel, out_shape=[jax.ShapeDtypeStruct((ROWS, WIDTH)...  138 us
    unnamed x2, local copies, waits for them, and re-layouts  3.62 us

profile of v3, /device:TPU:7, one launch (start us, length us, event | category | flops | bytes accessed | tf_op | source)
XLA Modules:
  0.0 147.8 jit_solution(8455812163312606557)
XLA Ops:
  0.6 1.3 broadcast_in_dim.9.gain_ref
  3.2 138.0 %pairs.1 = (bf16[192,1152]{1,0:T(8,128)(2,1)}, bf16[192,1152]{1,0:T(8,128)(2,1)}, f32[48,1152]{1,0:T(8,128)}, f32[1,1152]{1,0:T(1,128)}) custom-call(bf16[192,1152]{1,0:T(8,128)(2,1)} %bitcast.4, bf16[192,1152]{1,0:T(8,128)(2,1)} %bitcast.5, bf16[1152,1152]{1,0:T(8,128)(2,1)} %proj_ref.1, f32[1,1152]{1,0:T(1,128)} %broadcast_in_dim.9.gain_ref, ...), custom_call_target="tpu_custom_call" | custom-call | tf_op jit(solution)/shard_map/pairs/pallas_call | solution.py:487
  141.2 1.6 %constant_dynamic-slice_fusion = f32[36,1152]{1,0:T(8,128)} fusion(f32[48,1152]{1,0:T(8,128)} %get-tuple-element.10, s32[]{:T(128)S(6)} %select_n.11), kind=kLoop, calls=%fused_computation | loop fusion | bytes 331780 | tf_op jit(solution)/shard_map/dynamic_slice | solution.py:550
  142.9 1.3 reduce
  144.2 1.8 %copy.14 = bf16[192,1,1152]{2,0,1:T(8,128)(2,1)} copy(bf16[192,1,1152]{2,0,1:T(8,128)(2,1)} %bitcast.7) | data formatting | bytes 884736
  146.0 1.8 %copy.15 = bf16[192,1,1152]{2,0,1:T(8,128)(2,1)} copy(bf16[192,1,1152]{2,0,1:T(8,128)(2,1)} %bitcast.6) | data formatting | bytes 884736

commit v4 on v3

--- a/solution.py
+++ b/solution.py
@@ -12,13 +12,13 @@
 ROWS = 192
 GRAIN = 16
 GRAINS = ROWS // GRAIN
-CHUNKS = (4, 4, 3, 1)
-STARTS = (0, 4, 8, 11)
-COUNT = len(CHUNKS)
+CHUNKS = ((6, 6), (4, 4, 3, 1))
+STARTS = ((0, 6), (0, 4, 8, 11))
+OWN_COUNT, COUNT = len(CHUNKS[0]), len(CHUNKS[1])
 PAIRS = 3072
 TXT, IMG = 0, 1
 OWN, FAR = 0, 1
-WINDOW = 2
+IMAGES_AFTER = 1
 BLOCK_ROWS = 144
 PIECE = 48
 CUT = 512
@@ -67,14 +67,15 @@
 def row_sum(values):
     return jnp.sum(values, axis=-1, keepdims=True)
 
-ONWARD = (1, -1, 1, -1)
-TXT_OWN = ((5.3, 10.3, 13.0), (8.7, 13.7, 16.7), (11.2, 16.2, 19.0), (12.0, 17.0, 20.0))
-IMG_OWN = ((11.0, 20.0, 26.0, 30.0), (13.0, 23.0, 29.0, 33.0), (15.0, 26.0, 32.0, 36.0), (17.0, 28.0, 34.0, 39.0))
+ONWARD = ((1, -1), (1, -1, 1, -1))
+TXT_OWN = ((6.0, 22.0, 27.1), (11.0, 23.0, 33.0))
+IMG_OWN = ((16.0, 58.5, 63.1), (21.0, 58.6, 64.1))
 FAR_TIMES = (
-    ((24.0, 30.0, 35.0, 38.0), (36.0, 40.5, 44.0, 46.5), (44.5, 48.0, 51.0, 53.5), (47.0, 49.5, 52.0, 54.0)),
-    ((69.0, 74.0, 78.5, 81.0), (76.0, 80.5, 84.5, 87.5), (82.0, 85.5, 88.3, 90.0), (84.0, 87.0, 89.5, 91.0)),
+    ((27.0, 32.5, 36.0, 39.0), (34.0, 38.5, 42.5, 43.5), (38.6, 46.5, 49.0, 51.0), (42.6, 47.5, 50.0, 52.0)),
+    ((61.0, 68.0, 74.5, 80.6), (67.6, 73.0, 78.5, 87.5), (74.0, 80.5, 86.8, 90.0), (80.0, 86.5, 89.0, 91.0)),
 )
-TAIL = (55.0, 58.0, 60.0, 66.0, 67.0, 71.0, 72.0, 86.0, 89.2, 92.0)
+DRAINS = ((63.0, 0.6), (78.6, 0.8))
+TAIL = (53.0, 58.0, 60.0, 66.0, 67.0, 71.0, 72.0, 81.2, 86.0, 92.0)
 GAIN_TIMES = (62.5, 67.5, 72.2, 90.5, 92.5)
 
 
@@ -109,7 +110,7 @@
         return ((x + steps) % 4) * 2 + owner_core
 
     def block(arr, half, k, where):
-        return units.at[arr, half, pl.ds(STARTS[k], CHUNKS[k]), where]
+        return units.at[arr, half, pl.ds(STARTS[half][k], CHUNKS[half][k]), where]
 
     def x_copy(arr, half, k, steps, where, target):
         ref = block(arr, half, k, where)
@@ -120,7 +121,8 @@
         return remote(ref, ref, s_send.at[arr, half, k, steps], s_recv.at[arr, half, k, steps], sibling)
 
     def z_copy(arr, k):
-        return remote(block(arr, OWN, k, mine), block(arr, FAR, k, mine), z_send.at[arr, k], z_recv.at[arr, k], far)
+        src = units.at[arr, OWN, pl.ds(STARTS[FAR][k], CHUNKS[FAR][k]), mine]
+        return remote(src, block(arr, FAR, k, mine), z_send.at[arr, k], z_recv.at[arr, k], far)
 
     def recv_x(arr, half, k, steps):
         x_copy(arr, half, k, steps, slot(steps), plus).wait_recv()
@@ -133,7 +135,7 @@
     def spread_neighbours(arr, half, k):
         recv_x(arr, half, k, 3)
         recv_x(arr, half, k, 1)
-        if ONWARD[k] == 1:
+        if ONWARD[half][k] == 1:
             go(x_copy(arr, half, k, 2, slot(3), plus))
         else:
             go(x_copy(arr, half, k, 2, slot(1), minus))
@@ -147,7 +149,7 @@
     def attend(arr, half, k):
         for steps in range(4):
             s_copy(arr, half, k, steps, 1).wait_recv()
-        first, count = STARTS[k], CHUNKS[k]
+        first, count = STARTS[half][k], CHUNKS[half][k]
         own = units[1 - arr, OWN, :, mine].reshape(ROWS, WIDTH)
         keys = units[arr, half, pl.ds(first, count)].reshape(count * 8 * GRAIN, WIDTH)
         logits = scale * lax.dot_general(own, keys, LAST, preferred_element_type=F32) + bias
@@ -166,9 +168,7 @@
 
     def arrive(i):
         z_copy(*crossing[i]).wait_recv()
-        if i + WINDOW < COUNT:
-            go(z_copy(*crossing[i + WINDOW]))
-        if i == COUNT - 1:
+        if i == IMAGES_AFTER:
             for k in range(COUNT):
                 go(z_copy(IMG, k))
         spread_own(crossing[i][0], FAR, crossing[i][1])
@@ -196,9 +196,9 @@
     low, high = pl.ds(0, CUT), pl.ds(CUT, REST)
     here = y_rows(0)
 
-    def ya_copy(j, d):
+    def ya_copy(d):
         return remote(
-            summed.at[j, y_rows(d), low], ya_buf.at[d - 1, j], ya_send.at[d - 1, j], ya_recv.at[d - 1, j], y_peers[d - 1]
+            summed.at[:, y_rows(d), low], ya_buf.at[d - 1], ya_send.at[d - 1], ya_recv.at[d - 1], y_peers[d - 1]
         )
 
     def xb_copy(d):
@@ -211,9 +211,8 @@
             own = product(core, j)
             half_copy(j).wait_recv()
             summed[j] = (own + s_buf[j].astype(F32)).astype(BF16)
-            for d in (2, 1, 3):
-                go(ya_copy(j, d))
         for d in (2, 1, 3):
+            go(ya_copy(d))
             go(xb_copy(d))
 
     def norm_back():
@@ -223,7 +222,7 @@
         for i in range(9):
             g_sum[0, pl.ds(i, 1)] = terms[:, 128 * i : 128 * (i + 1)]
         go(g_copies(0)[0])
-        scaled = value * gain_ref[...]
+        scaled = value * gain_ref[...].reshape(1, WIDTH)
         mean = row_sum(scaled) * (1.0 / WIDTH)
         along = row_sum(scaled * xhat) * (1.0 / WIDTH)
         feature_out[...] = (row_ref[1][:, :1] * (scaled - mean - xhat * along)).astype(BF16)
@@ -244,10 +243,11 @@
             go(yb_copy(d))
 
     def second_sums_a():
+        for d in (1, 2, 3):
+            ya_copy(d).wait_recv()
         for j in range(4):
             total = summed[j, here, low].astype(F32)
             for d in (1, 2, 3):
-                ya_copy(j, d).wait_recv()
                 total = total + ya_buf[d - 1, j].astype(F32)
             ya_sum[j] = total.astype(BF16)
         for d in (2, 1, 3):
@@ -339,7 +339,11 @@
         def _():
             core_copy().start()
 
-        grad_out[...] = gathered[...].astype(F32)
+        for p in range(4):
+
+            @pl.when(y == p)
+            def _():
+                grad_out[...] = gathered[...].astype(F32)[4 * p : 4 * p + WIDTH // 32]
 
     stages = [([sibling], 0), (y_peers, 1), (x_peers, 4), (z_peers, 7)]
 
@@ -384,7 +388,7 @@
             g_core_copy().wait_recv()
 
         for i in range(9):
-            gain_out[:, pl.ds(128 * i, 128)] = g_sum[4, pl.ds(i, 1)]
+            gain_out[pl.ds(128 * i, 128)] = g_sum[4, i]
 
     def text_back():
         txt_back = acc[IMG]
@@ -406,7 +410,7 @@
         row_ref[1] = jnp.broadcast_to(deviation, (ROWS, 128))
         xhat = centred * deviation
         xhat_ref[...] = xhat
-        normed_ref[...] = (xhat * gain_ref[...]).astype(BF16)
+        normed_ref[...] = (xhat * gain_ref[...].reshape(1, WIDTH)).astype(BF16)
         projected = jnp.dot(normed_ref[...], proj_ref[...], preferred_element_type=F32)
         img_inv = lax.rsqrt(row_sum(projected * projected) + 1e-6)
         row_ref[2] = jnp.broadcast_to(img_inv, (ROWS, 128))
@@ -420,23 +424,25 @@
     acc[...] = jnp.zeros_like(acc)
     text_units()
     finish_barrier()
-    for i in range(WINDOW):
-        go(z_copy(*crossing[i]))
     for k in range(COUNT):
+        go(z_copy(TXT, k))
+    for k in range(OWN_COUNT):
         spread_own(TXT, OWN, k)
     image_units()
-
-    plan = [(9.0, transpose_normed, ())]
+    for k in range(OWN_COUNT):
+        spread_own(IMG, OWN, k)
+
+    plan = [(5.0, transpose_normed, ())]
 
     def chain(arr, half, k, neighbours, last, pairs):
         plan.append((neighbours, spread_neighbours, (arr, half, k)))
         plan.append((last, spread_last, (arr, half, k)))
         plan.append((pairs, attend, (arr, half, k)))
 
+    for k in range(OWN_COUNT):
+        chain(TXT, OWN, k, *TXT_OWN[k])
+        chain(IMG, OWN, k, *IMG_OWN[k])
     for k in range(COUNT):
-        chain(TXT, OWN, k, *TXT_OWN[k])
-        plan.append((IMG_OWN[k][0], spread_own, (IMG, OWN, k)))
-        chain(IMG, OWN, k, *IMG_OWN[k][1:])
         for arr in (TXT, IMG):
             times = FAR_TIMES[arr][k]
             plan.append((times[0], arrive, (arr * COUNT + k,)))
@@ -452,11 +458,17 @@
     plan.append((GAIN_TIMES[3], g_along_z, ()))
     plan.append((GAIN_TIMES[4], g_finish, ()))
     plan.append((200.0, text_back, ()))
+
+    def drain(fraction):
+        for _ in range(int(len(started) * fraction)):
+            started.pop(0).wait_send()
+
+    for time, fraction in DRAINS:
+        plan.append((time, drain, (fraction,)))
     for _, work, args in sorted(plan, key=lambda entry: entry[0]):
         work(*args)
 
-    for copy in started:
-        copy.wait_send()
+    drain(1.0)
     for half in (0, 1):
         away = away_from(half)
 
@@ -489,8 +501,8 @@
         out_shape=[
             jax.ShapeDtypeStruct((ROWS, WIDTH), BF16),
             jax.ShapeDtypeStruct((ROWS, WIDTH), BF16),
-            jax.ShapeDtypeStruct((PIECE, WIDTH), F32),
-            jax.ShapeDtypeStruct((1, WIDTH), F32),
+            jax.ShapeDtypeStruct((WIDTH // 32, WIDTH), F32),
+            jax.ShapeDtypeStruct((WIDTH,), F32),
         ],
         in_specs=[vmem] * 4 + [smem] * 2,
         out_specs=[vmem] * 4,
@@ -526,8 +538,8 @@
             dma((2, COUNT)),
             dma((4,)),
             dma((4,)),
-            dma((3, 4)),
-            dma((3, 4)),
+            dma((3,)),
+            dma((3,)),
             dma((3,)),
             dma((3,)),
             dma((3,)),
@@ -545,10 +557,8 @@
             collective_id=0, has_side_effects=True, vmem_limit_bytes=60 * 2**20
         ),
         name="pairs",
-    )(features[:, 0, :], text[:, 0, :], proj, gain[None, :], scale, bias)
-    y = lax.axis_index("rep") % 4
-    proj_grad = lax.dynamic_slice_in_dim(grad, y * 4, 36, 0)
-    return feature_grad[:, None, :], text_grad[:, None, :], proj_grad, gain_gradient[0]
+    )(features[:, 0, :], text[:, 0, :], proj, gain, scale, bias)
+    return feature_grad[:, None, :], text_grad[:, None, :], grad, gain_gradient
 
 def solution(mesh):
     return jax.shard_map(

time: 149 us -> 139 us (0.933)
  the two profiles are of different devices: /device:TPU:7 before, /device:TPU:33 now
where the time goes in v4:
time: 139 us
  Pallas kernels  131 us (94%)
  local copies, waits for them, and re-layouts  6.52 us (5%)
  between operations  1.93 us (1%)
    pallas_call x1, Pallas kernels, local(): pl.pallas_call(pair_kernel, out_shape=[jax.ShapeDtypeStruct((ROWS, WIDTH)...  131 us
    unnamed x4, local copies, waits for them, and re-layouts  6.52 us

profile of v4, /device:TPU:33, one launch (start us, length us, event | category | flops | bytes accessed | tf_op | source)
XLA Modules:
  0.0 139.0 jit_solution(16320929978699749302)
XLA Ops:
  1.9 130.5 %pairs.1 = (bf16[192,1152]{1,0:T(8,128)(2,1)}, bf16[192,1152]{1,0:T(8,128)(2,1)}, f32[36,1152]{1,0:T(8,128)}, f32[1152]{0:T(1024)}) custom-call(bf16[192,1152]{1,0:T(8,128)(2,1)} %bitcast.6, bf16[192,1152]{1,0:T(8,128)(2,1)} %bitcast.7, bf16[1152,1152]{1,0:T(8,128)(2,1)} %proj_ref.1, f32[1152]{0:T(1024)} %gain_ref.1, f32[1]{0:T(128)S(6)} %copy.14.scale_ref, ...), custom_call_target="tpu_custom_call" | custom-call | tf_op jit(solution)/shard_map/pairs/pallas_call | solution.py:499
  132.4 1.8 %copy.16 = bf16[192,1,1152]{2,0,1:T(8,128)(2,1)} copy(bf16[192,1,1152]{2,0,1:T(8,128)(2,1)} %bitcast.5) | data formatting | bytes 884736
  134.2 1.8 %copy.17 = bf16[192,1,1152]{2,0,1:T(8,128)(2,1)} copy(bf16[192,1,1152]{2,0,1:T(8,128)(2,1)} %bitcast.4) | data formatting | bytes 884736
  136.1 1.6 %copy.18 = f32[36,1152]{1,0:T(8,128)} copy(f32[36,1152]{1,0:T(8,128)} %get-tuple-element.18) | data formatting | bytes 331776
  137.7 1.3 copy.19

commit v5 on v4

--- a/solution.py
+++ b/solution.py
@@ -12,8 +12,8 @@
 ROWS = 192
 GRAIN = 16
 GRAINS = ROWS // GRAIN
-CHUNKS = ((6, 6), (4, 4, 3, 1))
-STARTS = ((0, 6), (0, 4, 8, 11))
+CHUNKS = ((6, 6), (5, 5, 2))
+STARTS = ((0, 6), (0, 5, 10))
 OWN_COUNT, COUNT = len(CHUNKS[0]), len(CHUNKS[1])
 PAIRS = 3072
 TXT, IMG = 0, 1
@@ -67,16 +67,16 @@
 def row_sum(values):
     return jnp.sum(values, axis=-1, keepdims=True)
 
-ONWARD = ((1, -1), (1, -1, 1, -1))
-TXT_OWN = ((6.0, 22.0, 27.1), (11.0, 23.0, 33.0))
-IMG_OWN = ((16.0, 58.5, 63.1), (21.0, 58.6, 64.1))
+ONWARD = ((1, -1), (1, -1, 1))
+TXT_OWN = ((6.0, 22.0, 30.5), (11.0, 23.0, 33.0))
+IMG_OWN = ((16.0, 61.0, 63.1), (21.0, 61.1, 64.1))
 FAR_TIMES = (
-    ((27.0, 32.5, 36.0, 39.0), (34.0, 38.5, 42.5, 43.5), (38.6, 46.5, 49.0, 51.0), (42.6, 47.5, 50.0, 52.0)),
-    ((61.0, 68.0, 74.5, 80.6), (67.6, 73.0, 78.5, 87.5), (74.0, 80.5, 86.8, 90.0), (80.0, 86.5, 89.0, 91.0)),
+    ((27.0, 32.0, 36.0, 39.5), (34.0, 39.0, 43.2, 47.5), (43.0, 46.0, 49.0, 50.0)),
+    ((67.4, 72.5, 76.0, 79.5), (72.3, 77.5, 81.0, 83.5), (77.0, 80.5, 84.0, 86.0)),
 )
 DRAINS = ((63.0, 0.6), (78.6, 0.8))
-TAIL = (53.0, 58.0, 60.0, 66.0, 67.0, 71.0, 72.0, 81.2, 86.0, 92.0)
-GAIN_TIMES = (62.5, 67.5, 72.2, 90.5, 92.5)
+TAIL = (53.0, 58.0, 60.0, 66.0, 67.0, 71.0, 72.0, 80.0, 83.0, 87.0)
+GAIN_TIMES = (62.5, 67.5, 72.2, 86.5, 88.0)
 
 
 def pair_kernel(
@@ -554,7 +554,7 @@
             dma((23,)),
         ],
         compiler_params=pltpu.CompilerParams(
-            collective_id=0, has_side_effects=True, vmem_limit_bytes=60 * 2**20
+            collective_id=0, has_side_effects=True, vmem_limit_bytes=34 * 2**20
         ),
         name="pairs",
     )(features[:, 0, :], text[:, 0, :], proj, gain, scale, bias)

time: 139 us -> 137 us (0.986)
  the two profiles are of different devices: /device:TPU:33 before, /device:TPU:105 now
where the time goes in v5:
time: 137 us
  Pallas kernels  128 us (93%)
  local copies, waits for them, and re-layouts  7.26 us (5%)
  between operations  1.95 us (1%)
    pallas_call x1, Pallas kernels, local(): pl.pallas_call(pair_kernel, out_shape=[jax.ShapeDtypeStruct((ROWS, WIDTH)...  128 us
    unnamed x12, local copies, waits for them, and re-layouts  7.26 us

profile of v5, /device:TPU:105, one launch (start us, length us, event | category | flops | bytes accessed | tf_op | source)
XLA Modules:
  0.0 137.0 jit_solution(5318246703346636156)
XLA Ops:
  1.9 0.0 copy-start
  1.9 1.7 %copy-done = bf16[1152,1152]{1,0:T(8,128)(2,1)S(1)} copy-done((bf16[1152,1152]{1,0:T(8,128)(2,1)S(1)}, bf16[1152,1152]{1,0:T(8,128)(2,1)}, u32[]{:S(2)}) %copy-start) | copy-done | bytes 2654232
  3.7 0.0 copy-start.1
  3.7 1.0 copy-done.1
  4.7 0.0 copy-start.2
  4.7 1.0 copy-done.2
  5.7 0.0 copy-start.3
  5.7 0.7 copy-done.3
  6.4 127.8 %pairs.1 = (bf16[192,1152]{1,0:T(8,128)(2,1)S(1)}, bf16[192,1152]{1,0:T(8,128)(2,1)S(1)}, f32[36,1152]{1,0:T(8,128)S(1)}, f32[1152]{0:T(1024)S(1)}) custom-call(bf16[192,1152]{1,0:T(8,128)(2,1)S(1)} %bitcast.6, bf16[192,1152]{1,0:T(8,128)(2,1)S(1)} %bitcast.7, bf16[1152,1152]{1,0:T(8,128)(2,1)S(1)} %copy-done, f32[1152]{0:T(1024)S(1)} %copy-done.3, ...), custom_call_target="tpu_custom_call" | custom-call | tf_op jit(solution)/shard_map/pairs/pallas_call | solution.py:499
  134.2 0.8 copy.16
  135.0 0.8 copy.17
  135.7 0.7 copy.18
  136.4 0.6 copy.19
Async XLA Ops:
  1.9 1.8 %copy-start = (bf16[1152,1152]{1,0:T(8,128)(2,1)S(1)}, bf16[1152,1152]{1,0:T(8,128)(2,1)}, u32[]{:S(2)}) copy-start(bf16[1152,1152]{1,0:T(8,128)(2,1)} %proj_ref.1) | copy-start | bytes 7962628
  3.7 1.0 copy-start.1
  4.7 1.0 copy-start.2
  5.7 0.7 copy-start.3

commit v6 on v5

--- a/solution.py
+++ b/solution.py
@@ -80,13 +80,13 @@
 
 
 def pair_kernel(
-    feat_ref, text_ref, proj_ref, gain_ref, scale_ref, bias_ref,
+    feat_hbm, text_hbm, proj_hbm, gain_ref, scale_ref, bias_ref,
     feature_out, text_out, grad_out, gain_out,
     units, acc, xhat_ref, normed_ref, normed_t, img_dir_ref, txt_dir_ref, row_ref, back_ref,
     theirs, summed, s_buf, ya_buf, ya_sum, xb_buf, xb_sum, xa_buf, yb_buf, part, z_buf, gathered, g_sum, g_buf,
     x_send, x_recv, s_send, s_recv, z_send, z_recv,
     c_send, c_recv, ya_send, ya_recv, xb_send, xb_recv, xa_send, xa_recv, yb_send, yb_recv,
-    h_send, h_recv, b_send, b_recv, g_send, g_recv,
+    h_send, h_recv, b_send, b_recv, g_send, g_recv, feat_ref, text_ref, proj_ref, load_sem,
 ):
     x, y, z, core = coordinates()
     mine = x * 2 + core
@@ -97,6 +97,12 @@
     z_peers = [device(x, y, z + d, core) for d in range(1, 16)]
     far = z_peers[7]
     finish_barrier = greet([sibling] + x_peers + y_peers + z_peers)
+    loads = [
+        pltpu.make_async_copy(src, dst, load_sem.at[i])
+        for i, (src, dst) in enumerate(((text_hbm, text_ref), (feat_hbm, feat_ref), (proj_hbm, proj_ref)))
+    ]
+    for load in loads:
+        load.start()
     scale = scale_ref[0]
     bias = bias_ref[0]
     started = []
@@ -422,12 +428,15 @@
         normed_t[...] = normed_ref[...].T
 
     acc[...] = jnp.zeros_like(acc)
+    loads[0].wait()
     text_units()
     finish_barrier()
     for k in range(COUNT):
         go(z_copy(TXT, k))
     for k in range(OWN_COUNT):
         spread_own(TXT, OWN, k)
+    loads[1].wait()
+    loads[2].wait()
     image_units()
     for k in range(OWN_COUNT):
         spread_own(IMG, OWN, k)
@@ -495,6 +504,7 @@
 def local(features, text, proj, gain, scale, bias):
     vmem = pl.BlockSpec(memory_space=pltpu.VMEM)
     smem = pl.BlockSpec(memory_space=pltpu.SMEM)
+    hbm = pl.BlockSpec(memory_space=pltpu.HBM)
     dma = pltpu.SemaphoreType.DMA
     feature_grad, text_grad, grad, gain_gradient = pl.pallas_call(
         pair_kernel,
@@ -504,7 +514,7 @@
             jax.ShapeDtypeStruct((WIDTH // 32, WIDTH), F32),
             jax.ShapeDtypeStruct((WIDTH,), F32),
         ],
-        in_specs=[vmem] * 4 + [smem] * 2,
+        in_specs=[hbm] * 3 + [vmem] + [smem] * 2,
         out_specs=[vmem] * 4,
         scratch_shapes=[
             pltpu.VMEM((2, 2, GRAINS, 8, GRAIN, WIDTH), BF16),
@@ -552,9 +562,13 @@
             dma((2,)),
             dma((23,)),
             dma((23,)),
+            pltpu.VMEM((ROWS, WIDTH), BF16),
+            pltpu.VMEM((ROWS, WIDTH), BF16),
+            pltpu.VMEM((WIDTH, WIDTH), BF16),
+            dma((3,)),
         ],
         compiler_params=pltpu.CompilerParams(
-            collective_id=0, has_side_effects=True, vmem_limit_bytes=34 * 2**20
+            collective_id=0, has_side_effects=True, vmem_limit_bytes=52 * 2**20
         ),
         name="pairs",
     )(features[:, 0, :], text[:, 0, :], proj, gain, scale, bias)

time: 137 us -> 136 us (level)
  the two profiles are of different devices: /device:TPU:105 before, /device:TPU:7 now
where the time goes in v6:
time: 136 us; the launch traced here: 133 us
  Pallas kernels  126 us (93%)
  local copies, waits for them, and re-layouts  5.51 us (4%)
  between operations  1.94 us (1%)
    pallas_call x1, Pallas kernels, local(): pl.pallas_call(pair_kernel, out_shape=[jax.ShapeDtypeStruct((ROWS, WIDTH)...  126 us
    unnamed x10, local copies, waits for them, and re-layouts  5.51 us

profile of v6, /device:TPU:7, one launch (start us, length us, event | category | flops | bytes accessed | tf_op | source)
XLA Modules:
  0.0 133.0 jit_solution(13962629769855002908)
XLA Ops:
  1.9 0.0 copy-start
  1.9 1.0 copy-done
  2.9 0.0 copy-start.1
  2.9 1.0 copy-done.1
  4.0 0.0 copy-start.2
  4.0 0.7 copy-done.2
  4.6 125.5 %pairs.1 = (bf16[192,1152]{1,0:T(8,128)(2,1)S(1)}, bf16[192,1152]{1,0:T(8,128)(2,1)S(1)}, f32[36,1152]{1,0:T(8,128)S(1)}, f32[1152]{0:T(1024)S(1)}) custom-call(bf16[192,1152]{1,0:T(8,128)(2,1)S(1)} %bitcast.6, bf16[192,1152]{1,0:T(8,128)(2,1)S(1)} %bitcast.7, bf16[1152,1152]{1,0:T(8,128)(2,1)} %proj_hbm.1, f32[1152]{0:T(1024)S(1)} %copy-done.2, ...), custom_call_target="tpu_custom_call" | custom-call | tf_op jit(solution)/shard_map/pairs/pallas_call | solution.py:509
  130.2 0.8 copy.16
  131.0 0.8 copy.17
  131.7 0.7 copy.18
  132.4 0.6 copy.19
Async XLA Ops:
  1.9 1.0 copy-start
  2.9 1.0 copy-start.1
  4.0 0.7 copy-start.2
